TPU v7x, 512 devices: a whole 4x4x16 slice. The times are simulated.
512 devices in a mesh: vis: 64 (over z, y_lo, core), facet: 8 (over x, y_hi).
Axes of the slice: x: 4, y: 4 (y_hi: 2, y_lo: 2; y = y_hi * 2 + y_lo), z: 16, core: 2. Of those that a mesh axis runs over, the one named last changes fastest.
Arguments:
- image: float32 [16384, 16384], P('vis', 'facet'), may hold values from 0 to 2
- observed: float32 [2, 1048576], P(None, ('vis', 'facet')), may hold values from -6 to 6
- weights: float32 [1048576], P(('vis', 'facet')), may hold values from 0.25 to 4
- row_cell: int32 [1048576], P(('vis', 'facet')), may hold values from 0 to 8
- col_cell: int32 [1048576], P(('vis', 'facet')), may hold values from 0 to 16376, as said below
- row_offset: int32 [1048576], P(('vis', 'facet')), may hold values from 0 to 15
- col_offset: int32 [1048576], P(('vis', 'facet')), may hold values from 0 to 15
- kernel: float32 [16, 8], replicated, may hold values from 0.1 to 1
- thresholds: float32 [2], replicated, may hold values from 0.02 to 0.4
Outputs:
- updated: float32 [16384, 16384], P('vis', 'facet')
Inputs may be any that keep to these rules, and one draw needn't show every extreme that they name: Visibilities arrive bucketed by uv column tile: on the device at facet index f, every col_cell lies in [f * 2048, (f + 1) * 2048), so a kernel reaches at most 7 columns into the next tile.
All inputs are finite; a program needn't handle non-finite values.
Results may differ from a plain program's by a relative error of at most 0.0003.
Values sent between devices are 32-bit elements; how exact they have to be, the bound alone decides.
A program may use at most 64 MiB of HBM per device.

v0:
```python
import math

import jax
import jax.numpy as jnp
from jax import lax
from jax.sharding import PartitionSpec as P

ROWS = 16


STEP = 0.5
SPLINE = (0.0625, 0.25, 0.375, 0.25, 0.0625)


def shifted(value, axis, by):
    length = lax.axis_size(axis)
    pairs = [(i, i + by) for i in range(length) if 0 <= i + by < length]
    return lax.ppermute(value, axis, pairs)


def padded(block, sides, width):
    for axis, dim in sides:
        count = lax.axis_size(axis)
        forward = [(i, i + 1) for i in range(count - 1)]
        backward = [(target, source) for source, target in forward]
        low = lax.ppermute(
            lax.slice_in_dim(block, block.shape[dim] - width, None, axis=dim), axis, forward
        )
        high = lax.ppermute(lax.slice_in_dim(block, 0, width, axis=dim), axis, backward)
        block = jnp.concatenate([low, block, high], axis=dim)
    return block


def row_tables(first_row, count, total, uv_rows):
    rows = first_row + jnp.arange(count, dtype=jnp.int32)
    freqs = total // 8 + jnp.arange(uv_rows, dtype=jnp.int32)
    turn = freqs[:, None] * rows[None, :] % total
    angle = 2.0 * math.pi / total * turn.astype(jnp.float32)
    return (jnp.cos(angle), jnp.sin(angle))


def dft_tables(radix, sign):
    total_len = radix * radix
    index = jnp.arange(radix, dtype=jnp.int32)
    small_turn = index[:, None] * index[None, :] % radix
    small_angle = sign * 2.0 * math.pi * small_turn.astype(jnp.float32) / radix
    twist_turn = index[:, None] * index[None, :] % total_len
    twist_angle = sign * 2.0 * math.pi * twist_turn.astype(jnp.float32) / total_len
    return (jnp.cos(small_angle), jnp.sin(small_angle), jnp.cos(twist_angle), jnp.sin(twist_angle))


def left_apply(table, block):
    return jnp.einsum("kn,rnm->rkm", table, block, precision=lax.Precision.HIGHEST)


def right_apply(block, table):
    return jnp.einsum("rkn,nm->rkm", block, table, precision=lax.Precision.HIGHEST)


def transform(real_part, imag_part, radix, sign):
    row_count = real_part.shape[0]
    small_cos, small_sin, twist_cos, twist_sin = dft_tables(radix, sign)
    input_re = real_part.reshape(row_count, radix, radix)
    input_im = imag_part.reshape(row_count, radix, radix)
    first_re = left_apply(small_cos, input_re) - left_apply(small_sin, input_im)
    first_im = left_apply(small_cos, input_im) + left_apply(small_sin, input_re)
    turned_re = first_re * twist_cos - first_im * twist_sin
    turned_im = first_re * twist_sin + first_im * twist_cos
    final_re = right_apply(turned_re, small_cos) - right_apply(turned_im, small_sin)
    final_im = right_apply(turned_re, small_sin) + right_apply(turned_im, small_cos)
    final_re = jnp.swapaxes(final_re, 1, 2).reshape(row_count, radix * radix) / radix
    final_im = jnp.swapaxes(final_im, 1, 2).reshape(row_count, radix * radix) / radix
    return (final_re, final_im)


def grid_block(table, kernel, row_cell, col_cell, row_offset, col_offset, observed, weights):
    strip_rows = table.shape[1] // 2
    width = kernel.shape[1]
    taps = jnp.arange(width, dtype=jnp.int32)
    options = jnp.arange(kernel.shape[0], dtype=jnp.int32)
    row_pick = (row_offset[:, None] == options[None, :]).astype(jnp.float32)
    col_pick = (col_offset[:, None] == options[None, :]).astype(jnp.float32)
    row_taps = jnp.dot(row_pick, kernel, precision=lax.Precision.HIGHEST)
    col_taps = jnp.dot(col_pick, kernel, precision=lax.Precision.HIGHEST)
    distance = jnp.arange(strip_rows, dtype=jnp.int32)[None, :] - row_cell[:, None]
    row_weight = jnp.sum(
        (distance[:, :, None] == taps[None, None, :]).astype(jnp.float32) * row_taps[:, None, :],
        axis=2,
    )
    columns = col_cell[:, None] + taps[None, :]
    picked = table[columns]
    folded = jnp.einsum("bc,bcr->br", col_taps, picked, precision=lax.Precision.HIGHEST)
    model_re = jnp.sum(folded[:, :strip_rows] * row_weight, axis=1)
    model_im = jnp.sum(folded[:, strip_rows:] * row_weight, axis=1)
    misfit_re = weights * (model_re - observed[0])
    misfit_im = weights * (model_im - observed[1])
    spread = jnp.concatenate(
        [row_weight * misfit_re[:, None], row_weight * misfit_im[:, None]], axis=1
    )
    values = col_taps[:, :, None] * spread[:, None, :]
    return (columns.reshape(-1), values.reshape(-1, 2 * strip_rows))


def smooth_valid(extended, dilation, out_rows, out_cols):
    across = (
        SPLINE[0] * extended[:, 0:out_cols]
        + SPLINE[1] * extended[:, dilation : dilation + out_cols]
        + SPLINE[2] * extended[:, 2 * dilation : 2 * dilation + out_cols]
        + SPLINE[3] * extended[:, 3 * dilation : 3 * dilation + out_cols]
        + SPLINE[4] * extended[:, 4 * dilation : 4 * dilation + out_cols]
    )
    return (
        SPLINE[0] * across[0:out_rows, :]
        + SPLINE[1] * across[dilation : dilation + out_rows, :]
        + SPLINE[2] * across[2 * dilation : 2 * dilation + out_rows, :]
        + SPLINE[3] * across[3 * dilation : 3 * dilation + out_rows, :]
        + SPLINE[4] * across[4 * dilation : 4 * dilation + out_rows, :]
    )


def on_device(
    image, observed, weights, row_cell, col_cell, row_offset, col_offset, kernel, thresholds
):
    band_rows, facet_cols = image.shape
    facets = lax.axis_size("facet")
    groups = lax.axis_size("vis")
    total_cols = facet_cols * facets
    radix = math.isqrt(total_cols)
    root = math.sqrt(total_cols)
    width = kernel.shape[1]
    shard_len = weights.shape[0]
    total_vis = shard_len * groups * facets
    first_row = lax.axis_index("vis") * band_rows
    first_col = lax.axis_index("facet") * facet_cols
    row_cos, row_sin = row_tables(first_row, band_rows, total_cols, ROWS)
    stacked_rows = jnp.concatenate([row_cos, -row_sin], axis=0)
    both_parts = jnp.dot(stacked_rows, image, precision=lax.Precision.HIGHEST) / root
    part_re = both_parts[:ROWS]
    part_im = both_parts[ROWS:]
    part_re, part_im = lax.psum((part_re, part_im), "vis")
    rows_re, rows_im = (
        lax.all_to_all(part_re, "facet", split_axis=0, concat_axis=1, tiled=True),
        lax.all_to_all(part_im, "facet", split_axis=0, concat_axis=1, tiled=True),
    )
    spec_re, spec_im = transform(rows_re, rows_im, radix, -1.0)
    spec_re, spec_im = (
        lax.all_to_all(spec_re, "facet", split_axis=1, concat_axis=0, tiled=True),
        lax.all_to_all(spec_im, "facet", split_axis=1, concat_axis=0, tiled=True),
    )
    stacked = jnp.stack([spec_re, spec_im])
    rim = shifted(stacked[:, :, : width - 1], "facet", -1)
    local = jnp.concatenate([stacked, rim], axis=2)
    table = jnp.concatenate([local[0].T, local[1].T], axis=1)
    col_local = col_cell - first_col
    block = math.gcd(shard_len, 2048)
    block_count = shard_len // block

    def accumulate(step_index, grid):
        columns, values = grid_block(
            table, kernel, row_cell, col_local, row_offset, col_offset, observed, weights
        )
        return grid.at[columns].add(values)

    grid = lax.fori_loop(
        0, block_count, accumulate, jnp.zeros((facet_cols + width - 1, 2 * ROWS), jnp.float32)
    )
    spill = shifted(grid[facet_cols:], "facet", 1)
    own = jnp.concatenate([grid[: width - 1] + spill, grid[width - 1 : facet_cols]], axis=0)
    sums_re = own[:, :ROWS].T
    sums_im = own[:, ROWS:].T
    sums_re, sums_im = lax.psum((sums_re, sums_im), "vis")
    rows_re, rows_im = (
        lax.all_to_all(sums_re, "facet", split_axis=0, concat_axis=1, tiled=True),
        lax.all_to_all(sums_im, "facet", split_axis=0, concat_axis=1, tiled=True),
    )
    back_re, back_im = transform(rows_re, rows_im, radix, 1.0)
    back_re, back_im = (
        lax.all_to_all(back_re, "facet", split_axis=1, concat_axis=0, tiled=True),
        lax.all_to_all(back_im, "facet", split_axis=1, concat_axis=0, tiled=True),
    )
    scale = total_cols / (4.0 * math.sqrt(total_vis)) / root
    back_both = jnp.concatenate([back_re, back_im], axis=0)
    gradient = jnp.dot(stacked_rows.T, back_both, precision=lax.Precision.HIGHEST) * scale
    coarse = image - STEP * gradient
    kept = jnp.zeros_like(coarse)
    level_count = thresholds.shape[0]
    for level_index in range(level_count):
        dilation = 2**level_index
        extended = padded(coarse, (("vis", 0), ("facet", 1)), 2 * dilation)
        smoother = smooth_valid(extended, dilation, band_rows, facet_cols)
        detail = coarse - smoother
        kept = kept + detail - jnp.clip(detail, -thresholds[level_index], thresholds[level_index])
        coarse = smoother
    return jax.nn.relu(kept + coarse)


def solution(mesh):
    return jax.shard_map(
        on_device,
        mesh=mesh,
        in_specs=(
            P("vis", "facet"),
            P(None, ("vis", "facet")),
            P(("vis", "facet")),
            P(("vis", "facet")),
            P(("vis", "facet")),
            P(("vis", "facet")),
            P(("vis", "facet")),
            P(),
            P(),
        ),
        out_specs=P("vis", "facet"),
        check_vma=False,
    )
```

profile of v0, /device:TPU:1, one launch (start us, length us, event | category | flops | bytes accessed | tf_op | source)
XLA Modules:
  0.0 1161.8 jit_solution(16578789326948389270)
XLA Ops:
  14.0 405.8 %all-reduce.7.cloned.1.call-done = (f32[8,2,2048]{2,1,0:T(2,128)}, f32[8,2,2048]{2,1,0:T(2,128)}) async-done(((f32[8,2,2048]{2,1,0:T(2,128)}, f32[8,2,2048]{2,1,0:T(2,128)}), (f32[8,2,2048]{2,1,0:T(2,128)}, f32[8,2,2048]{2,1,0:T(2,128)})) %all-reduce.7.cloned.1.call-update) | async-done | bytes 262160 | tf_op jit(solution)/shard_map/psum | solution.py:140
  419.9 6.1 all-to-all-start
  426.7 6.2 all-to-all-done
  437.0 6.0 all-to-all-done.1
  452.3 5.2 all-to-all-done.3
  462.0 5.6 all-to-all-done.2
  470.1 3.7 collective-permute-done
  474.1 54.8 %gather_fusion = f32[16384,32]{1,0:T(8,128)} fusion(f32[2055,32]{1,0:T(8,128)S(1)} %copy.152, s32[16384]{0:T(1024)S(1)} %broadcast_clamp_fusion), kind=kCustom, calls=%fused_computation | custom fusion | bytes 4259840 | tf_op jit(solution)/shard_map/while/body/eval_jaxpr/gather | solution.py:91
  529.0 12.6 %fusion.1 = f32[2048,32]{1,0:T(8,128)S(1)} fusion(f32[16384,32]{1,0:T(8,128)} %gather_fusion, f32[2048,8]{1,0:T(8,128)S(1)} %fusion.33), kind=kLoop, calls=%fused_computation.5 | loop fusion | flops 983040 | bytes 2424832
  543.0 95.8 %scatter_custom_fusion = f32[2055,32]{1,0:T(8,128)S(1)} fusion(s32[16384]{0:T(1024)S(1)} %bitcast.105, f32[2048,32]{1,0:T(8,128)S(1)} %copy.153, f32[16384]{0:T(1024)S(1)} %mul.436, f32[]{:T(128)} %constant.100.clone.1), kind=kCustom, calls=%fused_computation.3 | custom fusion | flops 1048576 | bytes 1377156 | tf_op jit(solution)/shard_map/while/body/eval_jaxpr/scatter-add | solution.py:162
  638.8 3.5 collective-permute-start.1
  644.8 404.1 %all-reduce.5.cloned.1.call-done = (f32[8,2,2048]{2,1,0:T(2,128)}, f32[8,2,2048]{2,1,0:T(2,128)}) async-done(((f32[8,2,2048]{2,1,0:T(2,128)}, f32[8,2,2048]{2,1,0:T(2,128)}), (f32[8,2,2048]{2,1,0:T(2,128)}, f32[8,2,2048]{2,1,0:T(2,128)})) %all-reduce.5.cloned.1.call-update) | async-done | bytes 262160 | tf_op jit(solution)/shard_map/psum | solution.py:171
  1049.0 6.1 all-to-all-start.4
  1055.8 6.2 all-to-all-done.4
  1062.0 3.6 all-to-all-start.5
  1066.3 5.8 all-to-all-done.5
  1081.4 5.2 all-to-all-done.6
  1090.1 6.6 all-to-all-done.7
  1098.8 4.4 collective-permute-start.2
  1103.2 3.9 collective-permute-start.3
  1115.2 5.6 collective-permute-done.5
  1132.2 5.4 collective-permute-start.8
  1140.9 4.1 collective-permute-done.9
  1149.9 5.0 add_maximum_fusion
  (151 shorter events, 74.7 us)
Async XLA Ops:
  6.5 413.3 %all-reduce.7.cloned.1.call-start = ((), (), s32[]{:S(2)}) async-start(), calls=%async_computation.9 | async-start | bytes 524288 | tf_op jit(solution)/shard_map/psum | solution.py:140
  419.9 13.1 %all-to-all-start = ((f32[8,2,2048]{2,1,0:T(2,128)}), f32[8,2,2048]{2,1,0:T(2,128)S(1)}, u32[]{:S(2)}, u32[]{:S(2)}) async-start(f32[8,2,2048]{2,1,0:T(2,128)} %get-tuple-element.28), calls=%async_computation | async-start | bytes 262144 | tf_op jit(solution)/shard_map/all_to_all | solution.py:142
  433.0 10.1 all-to-all-start.1
  444.8 16.1 %copy-start.12 = (s32[2048]{0:T(1024)S(1)}, s32[2048]{0:T(1024)}, u32[]{:S(2)}) copy-start(s32[2048]{0:T(1024)} %param.14) | copy-start | bytes 24580
  447.5 10.1 all-to-all-start.3
  457.5 10.1 all-to-all-start.2
  460.9 588.0 %all-reduce.5.cloned.1.call-start = ((), (), s32[]{:S(2)}) async-start(), calls=%async_computation.8 | async-start | bytes 524288 | tf_op jit(solution)/shard_map/psum | solution.py:171
  467.8 6.0 collective-permute-start
  638.8 4.3 collective-permute-start.1
  1049.0 13.1 %all-to-all-start.4 = ((f32[8,2,2048]{2,1,0:T(2,128)}), f32[8,2,2048]{2,1,0:T(2,128)S(1)}, u32[]{:S(2)}, u32[]{:S(2)}) async-start(f32[8,2,2048]{2,1,0:T(2,128)} %get-tuple-element.26), calls=%async_computation.4 | async-start | bytes 262144 | tf_op jit(solution)/shard_map/all_to_all | solution.py:173
  1062.0 10.1 all-to-all-start.5
  1074.5 22.3 %copy-start.5 = (f32[256,2048]{1,0:T(8,128)S(1)}, f32[256,2048]{1,0:T(8,128)}, u32[]{:S(2)}) copy-start(f32[256,2048]{1,0:T(8,128)} %param.9) | copy-start | bytes 6291460
  1076.5 10.1 all-to-all-start.6
  1086.6 10.1 all-to-all-start.7
  1098.8 22.9 %copy-start.1 = (f32[256,2048]{1,0:T(8,128)}, f32[256,2048]{1,0:T(8,128)S(1)}, u32[]{:S(2)}) copy-start(f32[256,2048]{1,0:T(8,128)S(1)} %fusion.4) | copy-start | bytes 6291460
  1098.8 8.3 collective-permute-start.2
  1103.2 5.1 collective-permute-start.3
  1108.7 6.5 collective-permute-start.4
  1112.0 8.9 collective-permute-start.5
  1124.7 4.4 collective-permute-start.6
  1126.6 12.6 %copy-start.11 = (f32[2]{0:T(128)S(1)}, f32[2]{0:T(128)}, u32[]{:S(2)}) copy-start(f32[2]{0:T(128)} %param.17) | copy-start | bytes 28
  1126.7 5.2 collective-permute-start.7
  1132.2 8.7 collective-permute-start.8
  1137.7 7.3 collective-permute-start.9
  (9 other events, 34.8 us)
Sparse Core Ops, SparseCore 0:
  11.3 408.5 all-reduce.6
  644.9 403.9 all-reduce.4
where the time goes:
time: 1170 us; the launch traced here: 1160 us
  waiting for transfers between devices  877 us (75%)
  other arithmetic  125 us (11%)
  local copies, waits for them, and re-layouts  66.9 us (6%)
  starting transfers between devices  61.9 us (5%)
  matrix products  15.7 us (1%)
  between operations  15.5 us (1%)
    psum x1, waiting for transfers between devices, on_device(): part_re, part_im = lax.psum((part_re, part_im), 'vis')  406 us
    psum x1, waiting for transfers between devices, on_device(): sums_re, sums_im = lax.psum((sums_re, sums_im), 'vis')  404 us
    scatter-add x1, other arithmetic, accumulate(): return grid.at[columns].add(values)  95.8 us
    gather x1, local copies, waits for them, and re-layouts, grid_block(): picked = table[columns]  54.8 us
  transfers between devices with their start and end apart: 20, of which 17 were waited for; matrix products, arithmetic and copies ran while one was open for 1% of the time, Pallas kernels for 0%

commit v1 on v0

v1 whole, which is shorter than its diff:
```python
import functools
import math

import jax
import jax.numpy as jnp
import numpy as np
from jax import lax
from jax.experimental import pallas as pl
from jax.experimental.pallas import tpu as pltpu
from jax.sharding import PartitionSpec as P

NPIX = 16384
ROWS = 16
BAND = 256
COLS = 2048
Z = 16
W = 4
F = 8
KW = 8
VDEV = 2048
TAPS = 15
STEP = 0.5
SPLINE = (0.0625, 0.25, 0.375, 0.25, 0.0625)
MESH = pl.DeviceIdType.MESH
HI = lax.Precision.HIGHEST
f32 = jnp.float32
bf16 = jnp.bfloat16


def turn(value, period):
    return 2.0 * np.pi * (np.asarray(value, np.int64) % period).astype(np.float64) / period


def forward_mix():
    f = np.arange(F)[:, None, None]
    l = (2 * np.arange(W)[:, None] + np.arange(2)[None, :])[None]
    f, l = np.broadcast_arrays(f, l)

    def row(j, b, im):
        ang = turn(8 * f * j + 8 * l * b + l * j, 64)
        c, s = np.cos(ang), np.sin(ang)
        pair = (c, s) if im == 0 else (-s, c)
        return np.stack(pair, axis=2).reshape(-1)

    def quarter(j, b, im):
        return row(j, b, 1) if im == 0 else -row(j, b, 0)

    out = np.zeros((W, 96, 128))
    for w in range(W):
        rows = []
        for b_lo in range(4):
            for kind in (row, quarter):
                for im in range(2):
                    for j2 in range(2):
                        for h in range(2):
                            rows.append(kind(2 * w + j2, 4 * h + b_lo, im))
        for kind in (row, quarter):
            for im in range(2):
                for j in range(8):
                    rows.append(kind(j, 0, im))
        out[w] = np.stack(rows)
    return out.astype(np.float32)


def forward_freqs():
    out = np.zeros((W, 48), np.int32)
    for w in range(W):
        rows = [
            8 * (4 * h + b_lo) + 2 * w + j2
            for b_lo in range(4)
            for _ in range(2)
            for j2 in range(2)
            for h in range(2)
        ]
        rows += [2048 + j for _ in range(2) for j in range(8)]
        out[w] = rows
    return out


def forward_last():
    m = np.arange(256)[:, None]
    a = np.tile(np.arange(32), 4)[None, :]
    ang = turn(m * a, 256)
    return (np.concatenate([np.cos(ang), np.sin(ang)], axis=0) / 128.0).astype(np.float32)


def backward_first():
    t = np.arange(256)[:, None]
    m = np.arange(256)[None, :]
    ang = turn(t * m, 256)
    return np.concatenate([np.cos(ang), np.sin(ang)], axis=0).astype(np.float32)


def backward_order():
    return [
        (2 * w + j2, 4 * h + b_lo, im)
        for b_lo in range(4)
        for w in range(W)
        for im in range(2)
        for j2 in range(2)
        for h in range(2)
    ]


def backward_twist():
    freq = np.array([j + 8 * b for j, b, _ in backward_order()])[:, None]
    ang = turn(freq * np.arange(256)[None, :], NPIX)
    return np.stack([np.cos(ang), np.sin(ang)]).astype(np.float32)


def backward_mix(scale):
    order = backward_order()
    j = np.array([o[0] for o in order])
    b = np.array([o[1] for o in order])
    im_in = np.array([o[2] for o in order])

    def row(f, l, im):
        ang = turn(8 * f * j + 8 * l * b + l * j, 64)
        c, s = np.cos(ang), np.sin(ang)
        if im == 0:
            return np.where(im_in == 0, c, -s)
        return np.where(im_in == 0, s, c)

    out = np.zeros((F * W, 24, 128))
    for f in range(F):
        for w in range(W):
            here = out[f * W + w]
            for copy in range(2):
                for im in range(2):
                    for l1 in range(2):
                        here[copy * 4 + im * 2 + l1] = row(f, 2 * w + l1, im)
            for im in range(2):
                here[8 + im] = row(f, 8, im)
                here[16 + im] = row(f, -1, im)
    return (out * scale).astype(np.float32)


def split(x):
    hi = x.astype(bf16)
    return hi, (x - hi.astype(f32)).astype(bf16)


def split_host(x):
    hi = x.astype(jnp.bfloat16)
    lo = (x - hi.astype(np.float64)).astype(jnp.bfloat16)
    return hi, lo


def row_waves():
    u = np.arange(ROWS)[:, None] + NPIX // 8
    ang = turn(u * np.arange(-8, BAND + 8)[None, :], NPIX)
    return np.concatenate([np.cos(ang), -np.sin(ang)], axis=0)


def smooth_rows(x, dilation):
    out = np.zeros_like(x)
    for s, weight in zip(range(-2, 3), SPLINE):
        out += weight * np.roll(x, -s * dilation, axis=1)
    return out


def gradient_tables():
    out = np.zeros((3, 3, BAND, 96), jnp.bfloat16)
    base = row_waves()
    inside = np.ones((3, BAND + 16))
    inside[0, :8] = 0
    inside[2, BAND + 8 :] = 0
    for edge in range(3):
        level = base
        for step in range(3):
            if step:
                level = smooth_rows(level * inside[edge], 2 ** (step - 1))
            hi, lo = split_host(level[:, 8 : 8 + BAND].T)
            out[edge, step] = np.concatenate([hi, hi, lo], axis=1)
    return out


def dot(a, b, precision=None):
    return jnp.dot(a, b, preferred_element_type=f32, precision=precision)


def position():
    v = lax.axis_index("vis")
    return v, v // W, v % W, lax.axis_index("facet")


def local_peer(v, z, w, f, d):
    return (z * W + (w + d) % W, f)


def depth_peer(v, z, w, f, d):
    return (((z + d) % Z) * W + w, f)


def plane_peer(v, z, w, f, d):
    return (z * W + (w + d % W) % W, (f + d // W) % F)


def meet(pos, depth, plane, extra=()):
    barrier = pltpu.get_barrier_semaphore()

    def greet(peer):
        pl.semaphore_signal(barrier, inc=1, device_id=peer, device_id_type=MESH)

    def along(count, where):
        def body(d, carry):
            greet(where(*pos, d))
            return carry

        lax.fori_loop(1, count, body, 0)

    along(Z, depth)
    along(F * W, plane)
    for peer in extra:
        greet(peer)
    return barrier, (Z - 1) + (F * W - 1) + len(extra)


def exchange(pos, count, where, src, dst, sems):
    def copy(d):
        return pltpu.make_async_remote_copy(
            src_ref=src(d),
            dst_ref=dst(d),
            send_sem=sems.at[0, d],
            recv_sem=sems.at[1, d],
            device_id=where(*pos, d),
            device_id_type=MESH,
        )

    def start():
        def body(d, carry):
            copy(d).start()
            return carry

        lax.fori_loop(1, count, body, 0)

    def wait_recv():
        def body(d, carry):
            copy(d).wait_recv()
            return carry

        lax.fori_loop(1, count, body, 0)

    def wait_send():
        def body(d, carry):
            copy(d).wait_send()
            return carry

        lax.fori_loop(1, count, body, 0)

    return start, wait_recv, wait_send


def rows8(ref, slot):
    return ref.at[pl.ds(pl.multiple_of(slot * 8, 8), 8)]


def rows128(ref, slot):
    return ref.at[pl.ds(pl.multiple_of(slot * 128, 128), 128)]


def forward_kernel(
    image, waves, mix, twist, last,
    x_out, rim_out, left_out, right_out, top_out, bottom_out,
    parts, near, summed, far, mine, gathered, block, blocks, rim_row, rims,
    pack, left, right, top, bottom,
    near_sem, far_sem, plane_sem, depth_sem, rim_sem, spread_sem, halo_sem,
):
    pos = position()
    v, z, w, f = pos
    vs = ((v + Z * W - 1) % (Z * W), v, (v + 1) % (Z * W))
    fs = ((f + F - 1) % F, f, (f + 1) % F)
    ring = [(vs[i], fs[k]) for i in range(3) for k in range(3) if (i, k) != (1, 1)]
    barrier, count = meet(pos, depth_peer, plane_peer, ring)

    table = waves[...]
    table_hi, table_lo = split(table)
    both = jnp.concatenate([table_hi, table_lo], axis=0)
    for tile in range(8):
        lanes = pl.ds(tile * 256, 256)
        hi, lo = split(image[:, lanes])
        first = dot(both, hi)
        value = first[:32] + first[32:] + dot(table_hi, lo)
        for half in range(2):
            c = (tile % 2) * 2 + half
            for im in range(2):
                parts[pl.ds((tile // 2) * 128 + im * 4 + c, 16, stride=8), :] = value[
                    im * 16 : im * 16 + 16, half * 128 : half * 128 + 128
                ]
    pack[0] = jnp.transpose(image[:, 0:128])[0:8]
    pack[1] = jnp.transpose(image[:, COLS - 128 : COLS])[120:128]
    pl.semaphore_wait(barrier, count)

    start, recv, send = exchange(
        pos, W, local_peer,
        lambda d: rows128(parts, (w + d) % W), lambda d: rows128(near, d - 1), near_sem,
    )
    start()
    halo = []

    def halo_copy(src, dst, peer):
        halo.append(
            pltpu.make_async_remote_copy(
                src_ref=src, dst_ref=dst, send_sem=halo_sem.at[0, len(halo)],
                recv_sem=halo_sem.at[1, len(halo)], device_id=peer, device_id_type=MESH,
            )
        )
        halo[-1].start()

    halo_copy(image.at[pl.ds(0, 8)], bottom, (vs[0], fs[1]))
    halo_copy(image.at[pl.ds(BAND - 8, 8)], top, (vs[2], fs[1]))
    halo_copy(pack.at[0], right.at[:, pl.ds(128, 256)], (vs[1], fs[0]))
    halo_copy(pack.at[1], left.at[:, pl.ds(128, 256)], (vs[1], fs[2]))
    halo_copy(pack.at[0, :, pl.ds(0, 128)], right.at[:, pl.ds(384, 128)], (vs[0], fs[0]))
    halo_copy(pack.at[0, :, pl.ds(128, 128)], right.at[:, pl.ds(0, 128)], (vs[2], fs[0]))
    halo_copy(pack.at[1, :, pl.ds(0, 128)], left.at[:, pl.ds(384, 128)], (vs[0], fs[2]))
    halo_copy(pack.at[1, :, pl.ds(128, 128)], left.at[:, pl.ds(0, 128)], (vs[2], fs[2]))
    recv()
    summed[...] = (
        (parts[pl.ds(pl.multiple_of(w * 128, 128), 128), :] + near[0:128])
        + (near[128:256] + near[256:384])
    )
    sends = [send]

    start, recv, send = exchange(
        pos, Z, depth_peer,
        lambda d: rows8(summed, (z + d) % Z), lambda d: rows8(far, d - 1), far_sem,
    )
    start()
    recv()
    sends.append(send)
    total = summed[pl.ds(pl.multiple_of(z * 8, 8), 8), :]
    for d in range(Z - 1):
        total = total + far[d * 8 : d * 8 + 8]
    mine[...] = total

    own = f * W + w
    start, recv, send = exchange(
        pos, F * W, plane_peer,
        lambda d: mine, lambda d: rows8(gathered, own), plane_sem,
    )
    start()
    gathered[pl.ds(pl.multiple_of(own * 8, 8), 8), :] = total
    sends.append(send)
    recv()

    wide = jnp.concatenate(
        [gathered[pl.ds(0, 128, stride=2), :], gathered[pl.ds(1, 128, stride=2), :]], axis=1
    )
    mixed = dot(mix[w], wide, HI)
    cos, sin = twist[0], twist[1]
    turned_a, turned_b = [], []
    for part in range(5):
        size = 16 if part == 4 else 8
        a = mixed[part * 16 : part * 16 + size]
        b = mixed[part * 16 + size : part * 16 + 2 * size]
        c = cos[part * 8 : part * 8 + size]
        s = sin[part * 8 : part * 8 + size]
        turned_a.append(a * c + b * s)
        turned_b.append(b * c - a * s)
    turned = jnp.concatenate(
        [jnp.concatenate(turned_a, axis=0), jnp.concatenate(turned_b, axis=0)], axis=1
    )
    spec = dot(turned, last[...], HI)
    group = lax.broadcasted_iota(jnp.int32, (8, 128), 1) // 32
    value = spec[0:8]
    for b_lo in range(1, 4):
        value = jnp.where(group == b_lo, spec[b_lo * 8 : b_lo * 8 + 8], value)
    block[...] = value
    diagonal = lax.broadcasted_iota(jnp.int32, (16, 128), 0) == lax.broadcasted_iota(
        jnp.int32, (16, 128), 1
    )
    edge = jnp.where(diagonal, jnp.broadcast_to(spec[32:48, 0:1], (16, 128)), 0.0)
    rim_row[...] = jnp.sum(edge, axis=0, keepdims=True)

    start, recv, send = exchange(
        pos, Z, depth_peer,
        lambda d: block, lambda d: rows8(blocks, w * Z + z), depth_sem,
    )
    start()
    rim_start, rim_recv, rim_send = exchange(
        pos, Z, depth_peer, lambda d: rim_row, lambda d: rims.at[z], rim_sem,
    )
    rim_start()
    blocks[pl.ds(pl.multiple_of((w * Z + z) * 8, 8), 8), :] = value
    rims[z] = rim_row[...]
    sends += [send, rim_send]
    recv()

    start, recv, send = exchange(
        pos, W, local_peer,
        lambda d: rows128(blocks, w), lambda d: rows128(blocks, w), spread_sem,
    )
    start()
    rim_recv()
    for copy in halo:
        copy.wait()
    left_out[...] = left[...]
    right_out[...] = right[...]
    top_out[...] = top[...]
    bottom_out[...] = bottom[...]
    sends.append(send)
    recv()
    x_out[...] = blocks[...]
    for r in range(16):
        rim_out[r : r + 1, :] = rims[r]
    for send in sends:
        send()


def grid_kernel(
    x, rim, kernel_t, observed, weights, row_cell, col_cell, row_offset, col_offset,
    g_out, edge_out,
    table_hi, table_lo, pick, values_hi, values_lo,
):
    first_col = lax.axis_index("facet") * COLS
    lane = lax.broadcasted_iota(jnp.int32, (32, 256), 1)
    lane_half = lax.broadcasted_iota(jnp.int32, (16, 128), 1)

    for j in range(8):
        w, j2 = j // 2, j % 2
        both = []
        for im in range(2):
            halves = [
                x[pl.ds(w * 128 + im * 4 + j2 * 2 + h, 16, stride=8), :] for h in range(2)
            ]
            both.append(jnp.concatenate(halves, axis=1))
        tile = jnp.concatenate(both, axis=0)
        hi, lo = split(tile)
        table_hi[j * 32 : j * 32 + 32, :] = hi
        table_lo[j * 32 : j * 32 + 32, :] = lo
        if j < 7:
            beyond = jnp.concatenate(
                [
                    jnp.broadcast_to(rim[:, im * 8 + j : im * 8 + j + 1], (16, 256))
                    for im in range(2)
                ],
                axis=0,
            )
            once = pltpu.roll(tile, 224, 1)
            twice = pltpu.roll(once, 255, 1)
            moved = jnp.where(lane < 224, once, jnp.where(lane == 255, beyond, twice))
            hi, lo = split(moved)
            table_hi[(j + 8) * 32 : (j + 9) * 32, :] = hi
            table_lo[(j + 8) * 32 : (j + 9) * 32, :] = lo

    taps = kernel_t[...]
    o_of = lax.broadcasted_iota(jnp.int32, (16, 256), 1) // 16
    s_of = lax.broadcasted_iota(jnp.int32, (16, 256), 1) % 16
    rep = (lax.broadcasted_iota(jnp.int32, (16, 256), 0) == o_of).astype(f32)
    spread = dot(taps, rep, HI)
    padded = jnp.concatenate([spread, jnp.zeros((8, 256), f32)], axis=0)
    tap_table = jnp.where(s_of == 0, padded, 0.0)
    for s in range(1, 9):
        tap_table = jnp.where(s_of == s, pltpu.roll(padded, s, 0), tap_table)
    tap_hi, tap_lo = split(tap_table)
    tap_both = jnp.concatenate([tap_hi, tap_lo], axis=0)

    down = lax.broadcasted_iota(jnp.int32, (256, 256), 0)

    def onehot(index):
        return jnp.where(down == index, 1.0, 0.0).astype(bf16)

    def visit(step, carry):
        lanes = pl.ds(pl.multiple_of(step * 256, 256), 256)
        col = col_cell[:, lanes] - first_col
        q = col // 8
        chosen = onehot((q % 8) * 32 + q // 8)
        pick[:, lanes] = chosen
        col_taps = dot(tap_both, onehot(col_offset[:, lanes] * 16 + col % 8))
        col_taps = col_taps[:16] + col_taps[16:]
        row_taps = dot(tap_both, onehot(row_offset[:, lanes] * 16 + row_cell[:, lanes]))
        row_taps = row_taps[:16] + row_taps[16:]
        picked = dot(table_hi[...], chosen) + dot(table_lo[...], chosen)
        folded = picked[0:32] * col_taps[0:1]
        for d in range(1, TAPS):
            folded = folded + picked[d * 32 : d * 32 + 32] * col_taps[d : d + 1]
        misfit = []
        for im in range(2):
            model = jnp.sum(folded[im * 16 : im * 16 + 16] * row_taps, axis=0, keepdims=True)
            misfit.append(
                row_taps * (weights[:, lanes] * (model - observed[im : im + 1, lanes]))
            )
        fan = jnp.concatenate(misfit, axis=0)
        for d in range(TAPS):
            hi, lo = split(fan * col_taps[d : d + 1])
            values_hi[d * 32 : d * 32 + 32, lanes] = hi
            values_lo[d * 32 : d * 32 + 32, lanes] = lo
        return carry

    lax.fori_loop(0, VDEV // 256, visit, 0)

    def scatter(values):
        return lax.dot_general(
            values[...], pick[...], (((1,), (1,)), ((), ())), preferred_element_type=f32
        )

    grid = scatter(values_hi) + scatter(values_lo)
    edge = [jnp.zeros((16, 128), f32)]
    for j in range(8):
        w, j2 = j // 2, j % 2
        tile = grid[j * 32 : j * 32 + 32]
        if j < 7:
            over = grid[(j + 8) * 32 : (j + 9) * 32]
            once = pltpu.roll(over, 32, 1)
            twice = pltpu.roll(once, 1, 1)
            tile = tile + jnp.where(lane >= 32, once, jnp.where(lane == 0, 0.0, twice))
            for im in range(2):
                last = over[im * 16 : im * 16 + 16, 255:256]
                edge.append(
                    jnp.where(lane_half == im * 8 + j, jnp.broadcast_to(last, (16, 128)), 0.0)
                )
        for im in range(2):
            for h in range(2):
                g_out[pl.ds(w * 128 + im * 4 + j2 * 2 + h, 16, stride=8), :] = tile[
                    im * 16 : im * 16 + 16, h * 128 : h * 128 + 128
                ]
    edge_out[...] = functools.reduce(jnp.add, edge)


def rotate(x, sign):
    groups = x.shape[0] // 8
    out = []
    for g in range(groups):
        out.append(pltpu.roll(x[g * 8 : g * 8 + 8], 4, 0) * sign)
    return jnp.concatenate(out, axis=0)


def backward_kernel(
    g, edge, first, twist, mix,
    b_out, margin_out,
    near, near_edge, summed, summed_edge, far, far_edge, mine, mine_edge,
    gathered, edges, block, blocks, margin, margins,
    near_sem, near_edge_sem, far_sem, far_edge_sem, plane_sem, edge_sem, depth_sem, margin_sem,
    spread_sem,
):
    pos = position()
    v, z, w, f = pos
    barrier, count = meet(pos, depth_peer, plane_peer)
    pl.semaphore_wait(barrier, count)

    start, recv, send = exchange(
        pos, W, local_peer,
        lambda d: rows128(g, (w + d) % W), lambda d: rows128(near, d - 1), near_sem,
    )
    start()
    edge_start, edge_recv, edge_send = exchange(
        pos, W, local_peer, lambda d: edge, lambda d: near_edge.at[d - 1], near_edge_sem,
    )
    edge_start()
    sends = [send, edge_send]
    recv()
    summed[...] = (
        (g[pl.ds(pl.multiple_of(w * 128, 128), 128), :] + near[0:128])
        + (near[128:256] + near[256:384])
    )
    start, recv, send = exchange(
        pos, Z, depth_peer,
        lambda d: rows8(summed, (z + d) % Z), lambda d: rows8(far, d - 1), far_sem,
    )
    start()
    edge_recv()
    edge_sum = edge[...] + near_edge[0] + near_edge[1] + near_edge[2]
    for r in range(16):
        summed_edge[r] = edge_sum[r : r + 1]
    edge_start, edge_recv, edge_send = exchange(
        pos, Z, depth_peer,
        lambda d: summed_edge.at[(z + d) % Z], lambda d: far_edge.at[d - 1], far_edge_sem,
    )
    edge_start()
    sends += [send, edge_send]
    recv()
    total = summed[pl.ds(pl.multiple_of(z * 8, 8), 8), :]
    for d in range(Z - 1):
        total = total + far[d * 8 : d * 8 + 8]
    mine[...] = total

    own = f * W + w
    start, recv, send = exchange(
        pos, F * W, plane_peer,
        lambda d: mine, lambda d: rows8(gathered, own), plane_sem,
    )
    start()
    gathered[pl.ds(pl.multiple_of(own * 8, 8), 8), :] = total
    edge_recv()
    edge_total = summed_edge[z]
    for d in range(Z - 1):
        edge_total = edge_total + far_edge[d]
    mine_edge[...] = edge_total

    def facet_peer(v, z, w, f, d):
        return (v, (f + d) % F)

    edge_start, edge_recv, edge_send = exchange(
        pos, F, facet_peer, lambda d: mine_edge, lambda d: edges.at[f], edge_sem,
    )
    edge_start()
    edges[f] = edge_total
    sends += [send, edge_send]
    edge_recv()
    recv()

    row_index = lax.broadcasted_iota(jnp.int32, (32, 128), 0)
    lane = lax.broadcasted_iota(jnp.int32, (32, 128), 1)
    target = ((row_index // 4) % 2) * 8 + 2 * (row_index // 8) + (row_index // 2) % 2
    wanted = (lane == target) & (row_index % 2 == 0)
    tiles = []
    for facet in range(F):
        tile = gathered[facet * 32 : facet * 32 + 32]
        if facet:
            spill = jnp.where(wanted, jnp.broadcast_to(edges[facet - 1], (32, 128)), 0.0)
            column = jnp.sum(spill, axis=1, keepdims=True)
            tile = tile + jnp.where(lane == 0, jnp.broadcast_to(column, (32, 128)), 0.0)
        tiles.append(tile)
    group = lane // 32
    moved = [
        [tile if s == 0 else pltpu.roll(tile, 32 * s, 1) for s in range(4)] for tile in tiles
    ]
    rows = []
    for b_lo in range(4):
        halves = []
        for half in range(2):
            value = moved[half * 4][(0 - b_lo) % 4]
            for k in range(1, 4):
                value = jnp.where(group == k, moved[half * 4 + k][(k - b_lo) % 4], value)
            halves.append(value)
        rows.append(jnp.concatenate(halves, axis=1))
    stack = jnp.concatenate(rows, axis=0)
    sign = jnp.where(lax.broadcasted_iota(jnp.int32, (8, 256), 0) < 4, -1.0, 1.0)
    operand = jnp.concatenate([stack, rotate(stack, sign)], axis=1)
    spun = dot(operand, first[...], HI)
    spun = spun * twist[0] + rotate(spun, sign) * twist[1]
    out = dot(mix[own], spun, HI)
    top = lax.broadcasted_iota(jnp.int32, (8, 128), 0) < 4
    value = jnp.where(top, out[0:8, 0:128], out[0:8, 128:256])
    block[...] = value
    low = lax.broadcasted_iota(jnp.int32, (8, 128), 1) < 64
    sides = jnp.where(low, out[8:16, 0:128], out[16:24, 128:256])
    margin[...] = sides[0:2]

    start, recv, send = exchange(
        pos, Z, depth_peer,
        lambda d: block, lambda d: rows8(blocks, w * Z + z), depth_sem,
    )
    start()
    margin_start, margin_recv, margin_send = exchange(
        pos, Z, depth_peer, lambda d: margin, lambda d: margins.at[z], margin_sem,
    )
    margin_start()
    blocks[pl.ds(pl.multiple_of((w * Z + z) * 8, 8), 8), :] = value
    margins[z] = margin[...]
    sends += [send, margin_send]
    recv()
    start, recv, send = exchange(
        pos, W, local_peer,
        lambda d: rows128(blocks, w), lambda d: rows128(blocks, w), spread_sem,
    )
    start()
    margin_recv()
    sends.append(send)
    for r in range(16):
        for im in range(2):
            margin_out[im * 16 + r : im * 16 + r + 1, :] = margins[r, im : im + 1, :]
    recv()
    b_out[...] = blocks[...]
    for send in sends:
        send()


def weigh(x, dilation, axis):
    n = x.shape[axis]
    near = pltpu.roll(x, dilation, axis) + pltpu.roll(x, n - dilation, axis)
    wide = pltpu.roll(x, 2 * dilation, axis) + pltpu.roll(x, n - 2 * dilation, axis)
    return SPLINE[2] * x + (SPLINE[1] * near + SPLINE[0] * wide)


EXT = COLS + 256
TALL = BAND + 16


def smooth_kernel(image, left, right, top, bottom, one, two, ext, across):
    v = lax.axis_index("vis")
    f = lax.axis_index("facet")
    low_row = jnp.where(v == 0, 8, 0)
    high_row = jnp.where(v == Z * W - 1, BAND + 8, TALL)
    low_col = jnp.where(f == 0, 128, 0)
    high_col = jnp.where(f == F - 1, COLS + 128, EXT)
    ext[8 : 8 + BAND, 128 : 128 + COLS] = image[...]
    ext[0:8, 128 : 128 + COLS] = jnp.where(low_row == 0, top[...], 0.0)
    ext[BAND + 8 : TALL, 128 : 128 + COLS] = jnp.where(high_row == TALL, bottom[...], 0.0)
    tall = lax.broadcasted_iota(jnp.int32, (TALL, 128), 0)
    rows_in = (tall >= low_row) & (tall < high_row)
    side = jnp.concatenate([jnp.zeros((120, 512), f32), left[...]], axis=0)
    side = jnp.transpose(side)[120 : 120 + TALL]
    ext[:, 0:128] = jnp.where(rows_in & (low_col == 0), side, 0.0)
    side = jnp.concatenate([right[...], jnp.zeros((120, 512), f32)], axis=0)
    side = jnp.transpose(side)[120 : 120 + TALL]
    ext[:, EXT - 128 : EXT] = jnp.where(rows_in & (high_col == EXT), side, 0.0)

    def level(dilation, out):
        def columns(step, carry):
            rows = pl.ds(pl.multiple_of(step * 8, 8), 8)
            across[rows, :] = weigh(ext[rows, :], dilation, 1)
            return carry

        lax.fori_loop(0, TALL // 8, columns, 0)

        def down(step, carry):
            lanes = pl.ds(pl.multiple_of(step * 128, 128), 128)
            value = weigh(across[:, lanes], dilation, 0)
            col = lax.broadcasted_iota(jnp.int32, (TALL, 128), 1) + step * 128
            inside = rows_in & (col >= low_col) & (col < high_col)
            ext[:, lanes] = jnp.where(inside, value, 0.0)
            return carry

        lax.fori_loop(0, EXT // 128, down, 0)
        out[...] = ext[8 : 8 + BAND, 128 : 128 + COLS]

    level(1, one)
    level(2, two)


def final_kernel(image, one, two, b, margin, phase, waves, thresholds, out):
    v = lax.axis_index("vis")
    f = lax.axis_index("facet")
    edge = jnp.where(v == 0, 0, jnp.where(v == Z * W - 1, 2, 1))
    parts = []
    for im in range(2):
        tiles = [margin[im * 16 : im * 16 + 16, :]]
        for tile in range(16):
            w, l1, mh = tile // 4, (tile // 2) % 2, tile % 2
            tiles.append(b[pl.ds(w * 128 + mh * 4 + im * 2 + l1, 16, stride=8), :])
        tiles.append(margin[im * 16 : im * 16 + 16, :])
        parts.append(jnp.concatenate(tiles, axis=1))
    cos, sin = phase[0:16, 0:1], phase[16:32, 0:1]
    col = lax.broadcasted_iota(jnp.int32, (32, EXT), 1)
    low_col = jnp.where(f == 0, 128, 122)
    high_col = jnp.where(f == F - 1, COLS + 128, COLS + 134)
    inside = (col >= low_col) & (col < high_col)
    back = jnp.concatenate(
        [parts[0] * cos - parts[1] * sin, parts[1] * cos + parts[0] * sin], axis=0
    )
    levels = [jnp.where(inside, back, 0.0)]
    for dilation in (1, 2):
        levels.append(jnp.where(inside, weigh(levels[-1], dilation, 1), 0.0))
    operands = []
    for value in levels:
        hi, lo = split(value[:, 128 : 128 + COLS])
        operands.append(jnp.concatenate([hi, lo, hi], axis=0))
    for tile in range(COLS // 256):
        lanes = slice(tile * 256, tile * 256 + 256)
        c0 = image[:, lanes] - dot(waves[edge, 0], operands[0][:, lanes])
        c1 = one[:, lanes] - dot(waves[edge, 1], operands[1][:, lanes])
        c2 = two[:, lanes] - dot(waves[edge, 2], operands[2][:, lanes])
        d0, d1 = c0 - c1, c1 - c2
        t0, t1 = thresholds[0], thresholds[1]
        kept = (d0 - jnp.clip(d0, -t0, t0)) + (d1 - jnp.clip(d1, -t1, t1))
        out[:, lanes] = jnp.maximum(kept + c2, 0.0)


def vmem(count):
    return [pl.BlockSpec(memory_space=pltpu.VMEM)] * count


def sds(*shape, dtype=f32):
    return jax.ShapeDtypeStruct(shape, dtype)


LIMIT = 48 * 1024 * 1024


def call(body, outs, ins, scratch, **params):
    return pl.pallas_call(
        body,
        out_shape=outs,
        in_specs=ins,
        out_specs=jax.tree.map(lambda _: pl.BlockSpec(memory_space=pltpu.VMEM), outs),
        scratch_shapes=scratch,
        compiler_params=pltpu.CompilerParams(vmem_limit_bytes=LIMIT, **params),
    )


def pairs(count):
    return pltpu.SemaphoreType.DMA((2, count))


def on_device(
    image, observed, weights, row_cell, col_cell, row_offset, col_offset, kernel, thresholds
):
    v = lax.axis_index("vis")
    w = v % W
    f = lax.axis_index("facet")
    root = math.sqrt(NPIX)
    m = jnp.arange(256, dtype=jnp.int32)
    u = NPIX // 8 + jnp.arange(ROWS, dtype=jnp.int32)
    angle = (2.0 * math.pi / NPIX) * (u[:, None] * (v * BAND + m)[None, :] % NPIX).astype(f32)
    waves = jnp.concatenate([jnp.cos(angle), -jnp.sin(angle)], axis=0)
    freq = lax.dynamic_index_in_dim(jnp.asarray(forward_freqs()), w, 0, False) + f * COLS
    angle = (2.0 * math.pi / NPIX) * (freq[:, None] * m[None, :] % NPIX).astype(f32)
    twist = jnp.stack([jnp.cos(angle), jnp.sin(angle)])
    angle = (2.0 * math.pi / NPIX) * (u * (v * BAND) % NPIX).astype(f32)
    phase = jnp.concatenate([jnp.cos(angle), jnp.sin(angle)])
    phase = jnp.broadcast_to(phase[:, None], (32, 128))

    V = pltpu.VMEM
    x, rim, left, right, top, bottom = call(
        forward_kernel,
        [sds(512, 128), sds(16, 128), sds(8, 512), sds(8, 512), sds(8, COLS), sds(8, COLS)],
        vmem(5),
        [
            V((512, 128), f32), V((384, 128), f32), V((128, 128), f32), V((120, 128), f32),
            V((8, 128), f32), V((256, 128), f32), V((8, 128), f32), V((512, 128), f32),
            V((1, 128), f32), V((16, 1, 128), f32),
            V((2, 8, 256), f32), V((8, 512), f32), V((8, 512), f32), V((8, COLS), f32),
            V((8, COLS), f32),
            pairs(W), pairs(Z), pairs(F * W), pairs(Z), pairs(Z), pairs(W), pairs(8),
        ],
        collective_id=0, has_side_effects=True,
    )(image, waves, jnp.asarray(forward_mix()), twist, jnp.asarray(forward_last() / 128.0))
    g, edge = call(
        grid_kernel,
        [sds(512, 128), sds(16, 128)],
        vmem(9),
        [V((480, 256), bf16), V((480, 256), bf16), V((256, VDEV), bf16),
         V((480, VDEV), bf16), V((480, VDEV), bf16)],
    )(
        x, rim, kernel.T, observed, weights[None], row_cell[None], col_cell[None],
        row_offset[None], col_offset[None],
    )
    scale = STEP * NPIX / (4.0 * math.sqrt(VDEV * Z * W * F)) / root / root
    b, margin = call(
        backward_kernel,
        [sds(512, 128), sds(32, 128)],
        vmem(5),
        [
            V((384, 128), f32), V((3, 16, 128), f32), V((128, 128), f32), V((16, 1, 128), f32),
            V((120, 128), f32), V((15, 1, 128), f32), V((8, 128), f32), V((1, 128), f32),
            V((256, 128), f32), V((8, 1, 128), f32), V((8, 128), f32), V((512, 128), f32),
            V((2, 128), f32), V((16, 2, 128), f32),
            pairs(W), pairs(W), pairs(Z), pairs(Z), pairs(F * W), pairs(F), pairs(Z), pairs(Z),
            pairs(W),
        ],
        collective_id=1, has_side_effects=True,
    )(
        g, edge, jnp.asarray(backward_first()), jnp.asarray(backward_twist()),
        jnp.asarray(backward_mix(scale)),
    )
    one, two = call(
        smooth_kernel,
        [sds(BAND, COLS), sds(BAND, COLS)],
        vmem(5),
        [V((TALL, EXT), f32), V((TALL, EXT), f32)],
    )(image, left, right, top, bottom)
    return call(
        final_kernel,
        sds(BAND, COLS),
        vmem(7) + [pl.BlockSpec(memory_space=pltpu.SMEM)],
        [],
    )(image, one, two, b, margin, phase, jnp.asarray(gradient_tables()), thresholds)


def solution(mesh):
    return jax.shard_map(
        on_device,
        mesh=mesh,
        in_specs=(
            P("vis", "facet"),
            P(None, ("vis", "facet")),
            P(("vis", "facet")),
            P(("vis", "facet")),
            P(("vis", "facet")),
            P(("vis", "facet")),
            P(("vis", "facet")),
            P(),
            P(),
        ),
        out_specs=P("vis", "facet"),
        check_vma=False,
    )
```

time: 1170 us -> 126 us (0.11)
  waiting for transfers between devices: 877 us -> 0 us
  other arithmetic: 125 us -> 1.35 us
  Pallas kernels: 0 us -> 119 us
  local copies, waits for them, and re-layouts: 66.9 us -> 4.91 us
  starting transfers between devices: 61.9 us -> 0 us
  matrix products: 15.7 us -> 0 us
  between operations: 15.5 us -> 0.25 us
    psum x2 -> x0, waiting for transfers between devices: 810 us -> none  [the longest x1 406 us: on_device(): part_re, part_im = lax.psum((part_re, part_im), 'vis')]
    pallas_call x0 -> x5, Pallas kernels: none -> 119 us  [the longest x1 52.5 us: on_device(): call(forward_kernel, [sds(512, 128), sds(16, 128), sds(8, 512), sds(8, 51...]
    scatter-add x1 -> x0, other arithmetic: 95.8 us -> none  [accumulate(): return grid.at[columns].add(values)]
    gather x1 -> x0, local copies, waits for them, and re-layouts: 54.8 us -> none  [grid_block(): picked = table[columns]]
    all_to_all x8 -> x0, waiting for transfers between devices: 46.9 us -> none  [the longest x1 6.6 us: on_device(): lax.all_to_all(back_im, 'facet', split_axis=1, concat_axis=0, tiled=True)]
    all_to_all x8 -> x0, starting transfers between devices: 32.7 us -> none  [the longest x1 6.13 us: on_device(): lax.all_to_all(sums_re, 'facet', split_axis=0, concat_axis=1, tiled=True)]
    ppermute x10 -> x0, starting transfers between devices: 29.2 us -> none  [the longest x4 15 us: padded(): lax.ppermute(lax.slice_in_dim(block, block.shape[dim] - width, None, axis...]
    ppermute x10 -> x0, waiting for transfers between devices: 19.7 us -> none  [the longest x4 13.7 us: padded(): lax.ppermute(lax.slice_in_dim(block, 0, width, axis=dim), axis, backward)]
  transfers between devices with their start and end apart: 20 -> 0, of which waited for: 17 -> 0; matrix products, arithmetic and copies ran while one was open for 1% -> 0% of each run, Pallas kernels for 0% -> 0%
where the time goes in v1:
time: 126 us; the launch traced here: 125 us
  Pallas kernels  119 us (94%)
  local copies, waits for them, and re-layouts  4.91 us (4%)
  other arithmetic  1.35 us (1%)
    pallas_call x1, Pallas kernels, on_device(): call(forward_kernel, [sds(512, 128), sds(16, 128), sds(8, 512), sds(8, 51...  52.5 us
    pallas_call x1, Pallas kernels, on_device(): call(backward_kernel, [sds(512, 128), sds(32, 128)], vmem(5), [V((384, 12...  40.2 us
    pallas_call x1, Pallas kernels, on_device(): call(smooth_kernel, [sds(BAND, COLS), sds(BAND, COLS)], vmem(5), [V((TALL...  15.4 us
    pallas_call x1, Pallas kernels, on_device(): call(grid_kernel, [sds(512, 128), sds(16, 128)], vmem(9), [V((480, 256),...  5.76 us
    pallas_call x1, Pallas kernels, on_device(): call(final_kernel, sds(BAND, COLS), vmem(7) + [pl.BlockSpec(memory_space=...  4.92 us
    unnamed x34, local copies, waits for them, and re-layouts  4.84 us

profile of v1, /device:TPU:1, one launch (start us, length us, event | category | flops | bytes accessed | tf_op | source)
XLA Modules:
  0.0 125.4 jit_solution(13134593874927913960)
XLA Ops:
  0.0 0.0 copy-start.13
  0.0 0.0 copy-start.12
  0.0 0.0 copy-start.11
  0.0 0.0 copy-start.10
  0.0 0.0 copy-start.9
  0.1 0.8 add_bitcast_fusion
  0.9 0.1 fusion.15
  0.9 0.1 pad_maximum_fusion.2
  1.0 0.1 broadcast_in_dim.30.phase
  1.1 0.2 fusion.11
  1.2 0.3 fusion.7
  1.5 0.0 copy-start
  1.5 1.6 %copy-done = f32[256,2048]{1,0:T(8,128)S(1)} copy-done((f32[256,2048]{1,0:T(8,128)S(1)}, f32[256,2048]{1,0:T(8,128)}, u32[]{:S(2)}) %copy-start) | copy-done | bytes 2097176
  3.1 0.9 copy-done.7
  4.1 0.9 copy-done.8
  5.0 52.5 %shard_map.154 = (f32[512,128]{1,0:T(8,128)S(1)}, f32[16,128]{1,0:T(8,128)S(1)}, f32[8,512]{1,0:T(8,128)S(1)}, f32[8,512]{1,0:T(8,128)S(1)}, f32[8,2048]{1,0:T(8,128)S(1)}, /*index=5*/f32[8,2048]{1,0:T(8,128)S(1)}) custom-call(f32[256,2048]{1,0:T(8,128)S(1)} %copy-done, f32[32,256]{1,0:T(8,128)S(1)} %pad_maximum_fusion.1.waves, f32[4,96,128]{2,1,0:T(8,128)S(1)} %copy-done.8, ...), custom_call_target="tpu_custom_call" | custom-call | tf_op jit(solution)/shard_map/pallas_call | solution.py:806
  57.6 0.0 copy-start.1
  57.6 0.0 copy-start.3
  57.6 0.0 copy-start.16
  57.7 5.8 %shard_map.156 = (f32[512,128]{1,0:T(8,128)S(1)}, f32[16,128]{1,0:T(8,128)S(1)}) custom-call(f32[512,128]{1,0:T(8,128)S(1)} %get-tuple-element.23.x, f32[16,128]{1,0:T(8,128)S(1)} %get-tuple-element.24.rim, f32[8,16]{1,0:T(8,128)S(1)} %bitcast.13, f32[2,2048]{1,0:T(2,128)S(1)} %copy-done.9, f32[1,2048]{1,0:T(1,128)S(1)} %bitcast.8, s32[1,2048]{1,0:T(1,128)S(1)} %bitcast.9, ...), custom_call_target="tpu_custom_call" | custom-call | tf_op jit(solution)/shard_map/pallas_call | solution.py:820
  63.5 40.2 %shard_map.157 = (f32[512,128]{1,0:T(8,128)S(1)}, f32[32,128]{1,0:T(8,128)S(1)}) custom-call(f32[512,128]{1,0:T(8,128)S(1)} %get-tuple-element.25.g, f32[16,128]{1,0:T(8,128)S(1)} %get-tuple-element.26.edge, f32[512,256]{1,0:T(8,128)S(1)} %copy-done.4, f32[2,128,256]{2,1,0:T(8,128)S(1)} %copy-done.6, f32[32,24,128]{2,1,0:T(8,128)S(1)} %copy-done.5), custom_call_target="tpu_custom_call" | custom-call | tf_op jit(solution)/shard_map/pallas_call | solution.py:831
  103.7 15.4 %shard_map.155 = (f32[256,2048]{1,0:T(8,128)S(1)}, f32[256,2048]{1,0:T(8,128)S(1)}) custom-call(f32[256,2048]{1,0:T(8,128)} %image.5, f32[8,512]{1,0:T(8,128)S(1)} %get-tuple-element.17.left, f32[8,512]{1,0:T(8,128)S(1)} %get-tuple-element.18.right, f32[8,2048]{1,0:T(8,128)S(1)} %get-tuple-element.19.top, f32[8,2048]{1,0:T(8,128)S(1)} %get-tuple-element.20.bottom), custom_call_target="tpu_custom_call" | custom-call | tf_op jit(solution)/shard_map/pallas_call | solution.py:848
  119.1 1.3 %copy-done.2 = f32[256,2048]{1,0:T(8,128)} copy-done((f32[256,2048]{1,0:T(8,128)}, f32[256,2048]{1,0:T(8,128)S(1)}, u32[]{:S(2)}) %copy-start.2) | copy-done | bytes 2097176
  120.4 4.9 %shard_map.158 = f32[256,2048]{1,0:T(8,128)} custom-call(f32[256,2048]{1,0:T(8,128)S(1)} %copy-done.1, f32[256,2048]{1,0:T(8,128)S(1)} %get-tuple-element.21.one, f32[256,2048]{1,0:T(8,128)} %copy-done.2, f32[512,128]{1,0:T(8,128)S(1)} %get-tuple-element.27.b, f32[32,128]{1,0:T(8,128)S(1)} %get-tuple-element.28.margin, ...), custom_call_target="tpu_custom_call" | custom-call | tf_op jit(solution)/shard_map/pallas_call | solution.py:854
  (25 shorter events, 0.1 us)
Async XLA Ops:
  0.0 63.4 %copy-start.5 = (f32[32,24,128]{2,1,0:T(8,128)S(1)}, f32[32,24,128]{2,1,0:T(8,128)}, u32[]{:S(2)}) copy-start(f32[32,24,128]{2,1,0:T(8,128)} %constant.84.clone.mix) | copy-start | bytes 1179652
  0.0 57.6 %copy-start.15 = (f32[16,8]{0,1:T(8,128)S(1)}, f32[16,8]{0,1:T(8,128)}, u32[]{:S(2)}) copy-start(f32[16,8]{0,1:T(8,128)} %param.23) | copy-start | bytes 1540
  0.0 57.6 %copy-start.14 = (s32[2048]{0:T(1024)S(1)}, s32[2048]{0:T(1024)}, u32[]{:S(2)}) copy-start(s32[2048]{0:T(1024)} %param.22) | copy-start | bytes 24580
  0.0 57.6 %copy-start.13 = (s32[2048]{0:T(1024)S(1)}, s32[2048]{0:T(1024)}, u32[]{:S(2)}) copy-start(s32[2048]{0:T(1024)} %param.21) | copy-start | bytes 24580
  0.0 57.6 %copy-start.12 = (s32[2048]{0:T(1024)S(1)}, s32[2048]{0:T(1024)}, u32[]{:S(2)}) copy-start(s32[2048]{0:T(1024)} %param.20) | copy-start | bytes 24580
  0.0 57.6 %copy-start.11 = (s32[2048]{0:T(1024)S(1)}, s32[2048]{0:T(1024)}, u32[]{:S(2)}) copy-start(s32[2048]{0:T(1024)} %param.19) | copy-start | bytes 24580
  0.0 57.6 %copy-start.10 = (f32[2048]{0:T(1024)S(1)}, f32[2048]{0:T(1024)}, u32[]{:S(2)}) copy-start(f32[2048]{0:T(1024)} %param.18) | copy-start | bytes 24580
  0.0 57.6 %copy-start.9 = (f32[2,2048]{1,0:T(2,128)S(1)}, f32[2,2048]{1,0:T(2,128)}, u32[]{:S(2)}) copy-start(f32[2,2048]{1,0:T(2,128)} %observed.1) | copy-start | bytes 49156
  1.5 1.6 %copy-start = (f32[256,2048]{1,0:T(8,128)S(1)}, f32[256,2048]{1,0:T(8,128)}, u32[]{:S(2)}) copy-start(f32[256,2048]{1,0:T(8,128)} %image.5) | copy-start | bytes 6291460
  3.1 0.9 copy-start.7
  4.1 0.9 copy-start.8
  5.0 58.4 %copy-start.4 = (f32[512,256]{1,0:T(8,128)S(1)}, f32[512,256]{1,0:T(8,128)}, u32[]{:S(2)}) copy-start(f32[512,256]{1,0:T(8,128)} %constant.82.clone.first) | copy-start | bytes 1572868
  5.0 58.4 %copy-start.6 = (f32[2,128,256]{2,1,0:T(8,128)S(1)}, f32[2,128,256]{2,1,0:T(8,128)}, u32[]{:S(2)}) copy-start(f32[2,128,256]{2,1,0:T(8,128)} %constant.83.clone.twist) | copy-start | bytes 786436
  57.6 62.9 %copy-start.1 = (f32[256,2048]{1,0:T(8,128)S(1)}, f32[256,2048]{1,0:T(8,128)}, u32[]{:S(2)}) copy-start(f32[256,2048]{1,0:T(8,128)} %image.5) | copy-start | bytes 6291460
  57.6 62.9 %copy-start.3 = (bf16[3,3,256,96]{3,2,1,0:T(8,128)(2,1)S(1)}, bf16[3,3,256,96]{3,2,1,0:T(8,128)(2,1)}, u32[]{:S(2)}) copy-start(bf16[3,3,256,96]{3,2,1,0:T(8,128)(2,1)} %constant.85.clone.waves) | copy-start | bytes 1327108
  57.6 62.9 %copy-start.16 = (f32[2]{0:T(128)S(1)}, f32[2]{0:T(128)}, u32[]{:S(2)}) copy-start(f32[2]{0:T(128)} %thresholds.1) | copy-start | bytes 28
  119.1 1.3 %copy-start.2 = (f32[256,2048]{1,0:T(8,128)}, f32[256,2048]{1,0:T(8,128)S(1)}, u32[]{:S(2)}) copy-start(f32[256,2048]{1,0:T(8,128)S(1)} %get-tuple-element.22.two) | copy-start | bytes 6291460

commit v2 on v1

v2 whole, which is shorter than its diff:
```python
import functools
import math

import jax
import jax.numpy as jnp
import numpy as np
from jax import lax
from jax.experimental import pallas as pl
from jax.experimental.pallas import tpu as pltpu
from jax.sharding import PartitionSpec as P

NPIX = 16384
ROWS = 16
BAND = 256
COLS = 2048
Z = 16
W = 4
F = 8
KW = 8
VDEV = 2048
TAPS = 15
STEP = 0.5
SPLINE = (0.0625, 0.25, 0.375, 0.25, 0.0625)
MESH = pl.DeviceIdType.MESH
HI = lax.Precision.HIGHEST
f32 = jnp.float32
bf16 = jnp.bfloat16


def turn(value, period):
    return 2.0 * np.pi * (np.asarray(value, np.int64) % period).astype(np.float64) / period


def forward_mix():
    f = np.arange(F)[:, None, None]
    l = (2 * np.arange(W)[:, None] + np.arange(2)[None, :])[None]
    f, l = np.broadcast_arrays(f, l)

    def row(j, b, im):
        ang = turn(8 * f * j + 8 * l * b + l * j, 64)
        c, s = np.cos(ang), np.sin(ang)
        pair = (c, s) if im == 0 else (-s, c)
        return np.stack(pair, axis=2).reshape(-1)

    def quarter(j, b, im):
        return row(j, b, 1) if im == 0 else -row(j, b, 0)

    out = np.zeros((W, 96, 128))
    for w in range(W):
        rows = []
        for b_lo in range(4):
            for kind in (row, quarter):
                for im in range(2):
                    for j2 in range(2):
                        for h in range(2):
                            rows.append(kind(2 * w + j2, 4 * h + b_lo, im))
        for kind in (row, quarter):
            for im in range(2):
                for j in range(8):
                    rows.append(kind(j, 0, im))
        out[w] = np.stack(rows)
    return out.astype(np.float32)


def forward_freqs():
    out = np.zeros((W, 48), np.int32)
    for w in range(W):
        rows = [
            8 * (4 * h + b_lo) + 2 * w + j2
            for b_lo in range(4)
            for _ in range(2)
            for j2 in range(2)
            for h in range(2)
        ]
        rows += [2048 + j for _ in range(2) for j in range(8)]
        out[w] = rows
    return out


def forward_last():
    m = np.arange(256)[:, None]
    a = np.tile(np.arange(32), 4)[None, :]
    ang = turn(m * a, 256)
    return (np.concatenate([np.cos(ang), np.sin(ang)], axis=0) / 128.0).astype(np.float32)


def backward_first():
    t = np.arange(256)[:, None]
    m = np.arange(256)[None, :]
    ang = turn(t * m, 256)
    return np.concatenate([np.cos(ang), np.sin(ang)], axis=0).astype(np.float32)


def backward_order():
    return [
        (2 * w + j2, 4 * h + b_lo, im)
        for b_lo in range(4)
        for w in range(W)
        for im in range(2)
        for j2 in range(2)
        for h in range(2)
    ]


def backward_twist():
    freq = np.array([j + 8 * b for j, b, _ in backward_order()])[:, None]
    ang = turn(freq * np.arange(256)[None, :], NPIX)
    return np.stack([np.cos(ang), np.sin(ang)]).astype(np.float32)


def backward_mix(scale):
    order = backward_order()
    j = np.array([o[0] for o in order])
    b = np.array([o[1] for o in order])
    im_in = np.array([o[2] for o in order])

    def row(f, l, im):
        ang = turn(8 * f * j + 8 * l * b + l * j, 64)
        c, s = np.cos(ang), np.sin(ang)
        if im == 0:
            return np.where(im_in == 0, c, -s)
        return np.where(im_in == 0, s, c)

    out = np.zeros((F * W, 24, 128))
    for f in range(F):
        for w in range(W):
            here = out[f * W + w]
            for copy in range(2):
                for im in range(2):
                    for l1 in range(2):
                        here[copy * 4 + im * 2 + l1] = row(f, 2 * w + l1, im)
            for im in range(2):
                here[8 + im] = row(f, 8, im)
                here[16 + im] = row(f, -1, im)
    return (out * scale).astype(np.float32)


def split(x):
    hi = x.astype(bf16)
    return hi, (x - hi.astype(f32)).astype(bf16)


def split_host(x):
    hi = x.astype(jnp.bfloat16)
    lo = (x - hi.astype(np.float64)).astype(jnp.bfloat16)
    return hi, lo


def row_waves():
    u = np.arange(ROWS)[:, None] + NPIX // 8
    ang = turn(u * np.arange(-8, BAND + 8)[None, :], NPIX)
    return np.concatenate([np.cos(ang), -np.sin(ang)], axis=0)


def smooth_rows(x, dilation):
    out = np.zeros_like(x)
    for s, weight in zip(range(-2, 3), SPLINE):
        out += weight * np.roll(x, -s * dilation, axis=1)
    return out


def gradient_tables():
    out = np.zeros((3, 3, BAND, 96), jnp.bfloat16)
    base = row_waves()
    inside = np.ones((3, BAND + 16))
    inside[0, :8] = 0
    inside[2, BAND + 8 :] = 0
    for edge in range(3):
        level = base
        for step in range(3):
            if step:
                level = smooth_rows(level * inside[edge], 2 ** (step - 1))
            hi, lo = split_host(level[:, 8 : 8 + BAND].T)
            out[edge, step] = np.concatenate([hi, hi, lo], axis=1)
    return out


def dot(a, b, precision=None):
    return jnp.dot(a, b, preferred_element_type=f32, precision=precision)


def position():
    v = lax.axis_index("vis")
    return v, v // W, v % W, lax.axis_index("facet")


def band_waves():
    rows = np.arange(Z * W)[:, None] * BAND + np.arange(BAND)[None, :]
    u = NPIX // 8 + np.arange(ROWS)
    ang = turn(u[None, :, None] * rows[:, None, :], NPIX)
    return np.concatenate([np.cos(ang), -np.sin(ang)], axis=1).astype(np.float32)


def forward_twist():
    freq = np.arange(F)[:, None, None] * COLS + forward_freqs()[None]
    ang = turn(freq.reshape(F * W, 48, 1) * np.arange(256), NPIX)
    return np.stack([np.cos(ang), np.sin(ang)], axis=1).astype(np.float32)


def band_phases():
    u = NPIX // 8 + np.arange(ROWS)
    ang = turn(u[None, :] * (np.arange(Z * W)[:, None] * BAND), NPIX)
    both = np.concatenate([np.cos(ang), np.sin(ang)], axis=1)
    return np.broadcast_to(both[:, :, None], (Z * W, 32, 128)).astype(np.float32)


def loop(count, body):
    def step(i, carry):
        body(i)
        return carry

    lax.fori_loop(0, count, step, 0)


def far_first(i):
    k = (i + 1) // 2
    return 8 + k - 2 * k * (i % 2)


FACETS_FAR_FIRST = (3, 5, 1, 7, 4, 2, 6, 0)


def rows8(ref, slot):
    return ref.at[pl.ds(pl.multiple_of(slot * 8, 8), 8)]


class Links:
    def __init__(self):
        self.v, self.z, self.w, self.f = position()
        self.pending = []

    def local(self, d):
        return (self.z * W + (self.w + d) % W, self.f)

    def depth(self, d):
        return (((self.z + d) % Z) * W + self.w, self.f)

    def plane(self, df, dw):
        return (self.z * W + (self.w + dw) % W, (self.f + df) % F)

    def copy(self, src, dst, sems, slot, peer):
        return pltpu.make_async_remote_copy(
            src_ref=src, dst_ref=dst, send_sem=sems.at[0, slot], recv_sem=sems.at[1, slot],
            device_id=peer, device_id_type=MESH,
        )

    def greet(self, extra):
        barrier = pltpu.get_barrier_semaphore()

        def signal(peer):
            pl.semaphore_signal(barrier, inc=1, device_id=peer, device_id_type=MESH)

        loop(Z - 1, lambda i: signal(self.depth(far_first(i))))
        for df in FACETS_FAR_FIRST:
            first = 0 if df else 1
            loop(W - first, lambda i: signal(self.plane(df, i + first)))
        for peer in extra:
            signal(peer)
        count = (Z - 1) + (F * W - 1) + len(extra)
        return lambda: pl.semaphore_wait(barrier, count)

    def later(self, wait):
        self.pending.append(wait)

    def finish(self):
        for wait in self.pending:
            wait()

    def reduce_rows(self, parts, near, near_sem, summed, far, far_sem):
        def near_copy(row, d):
            here = ((self.w + d) % W) * Z + row
            return self.copy(
                rows8(parts, here), rows8(near, (d - 1) * Z + row), near_sem,
                (d - 1) * Z + row, self.local(d),
            )

        def far_copy(d):
            row = (self.z + d) % Z
            return self.copy(rows8(summed, row), rows8(far, d), far_sem, d, self.depth(d))

        def send_row(row):
            for d in range(1, W):
                near_copy(row, d).start()

        def sum_row(row):
            for d in range(1, W):
                near_copy(row, d).wait_recv()
            value = parts[pl.ds(pl.multiple_of((self.w * Z + row) * 8, 8), 8), :]
            for d in range(1, W):
                value = value + near[
                    pl.ds(pl.multiple_of(((d - 1) * Z + row) * 8, 8), 8), :
                ]
            summed[pl.ds(pl.multiple_of(row * 8, 8), 8), :] = value

        loop(Z - 1, lambda i: send_row((self.z + far_first(i)) % Z))
        send_row(self.z)

        def forward():
            def step(i):
                d = far_first(i)
                sum_row((self.z + d) % Z)
                far_copy(d).start()

            loop(Z - 1, step)
            sum_row(self.z)

        def result():
            loop(Z - 1, lambda i: far_copy(i + 1).wait_recv())
            value = summed[pl.ds(pl.multiple_of(self.z * 8, 8), 8), :]
            for d in range(1, Z):
                value = value + far[d * 8 : d * 8 + 8]
            return value

        def done(row):
            for d in range(1, W):
                near_copy(row, d).wait_send()

        self.later(lambda: loop(Z, done))
        self.later(lambda: loop(Z - 1, lambda i: far_copy(i + 1).wait_send()))
        return forward, result

    def share_plane(self, mine, gathered, sem):
        own = self.f * W + self.w

        def each(act):
            for df in FACETS_FAR_FIRST:
                first = 0 if df else 1
                loop(
                    W - first,
                    lambda i: act(
                        self.copy(
                            mine, rows8(gathered, own), sem, df * W + i + first,
                            self.plane(df, i + first),
                        )
                    ),
                )

        each(lambda c: c.start())
        gathered[pl.ds(pl.multiple_of(own * 8, 8), 8), :] = mine[...]
        self.later(lambda: each(lambda c: c.wait_send()))
        return lambda: each(lambda c: c.wait_recv())

    def spread(self, block, blocks, depth_sem, local_sem):
        def depth_copy(d):
            return self.copy(
                block, rows8(blocks, self.w * Z + self.z), depth_sem, d, self.depth(d)
            )

        def local_copy(row, d):
            slot = self.w * Z + row
            return self.copy(
                rows8(blocks, slot), rows8(blocks, slot), local_sem, (d - 1) * Z + row,
                self.local(d),
            )

        def pass_on(row):
            for d in range(1, W):
                local_copy(row, d).start()

        loop(Z - 1, lambda i: depth_copy(far_first(i)).start())
        blocks[pl.ds(pl.multiple_of((self.w * Z + self.z) * 8, 8), 8), :] = block[...]
        pass_on(self.z)

        def relay():
            def step(i):
                d = far_first(Z - 2 - i)
                depth_copy(d).wait_recv()
                pass_on((self.z - d + Z) % Z)

            loop(Z - 1, step)

            def arrived(row):
                for d in range(1, W):
                    local_copy(row, d).wait_recv()

            loop(Z, arrived)

        def done(row):
            for d in range(1, W):
                local_copy(row, d).wait_send()

        self.later(lambda: loop(Z - 1, lambda i: depth_copy(i + 1).wait_send()))
        self.later(lambda: loop(Z, done))
        return relay

    def each_depth(self, src, dst, sem):
        def make(d):
            return self.copy(src(d), dst(d), sem, d, self.depth(d))

        loop(Z - 1, lambda i: make(far_first(i)).start())
        self.later(lambda: loop(Z - 1, lambda i: make(i + 1).wait_send()))
        return lambda: loop(Z - 1, lambda i: make(i + 1).wait_recv())


EXT = COLS + 256
TALL = BAND + 16
CHUNKS = 4


def main_kernel(
    image, waves_all, mix_all, twist_all, last_hbm, first_hbm, turn_hbm, unmix_all,
    kernel_t, observed, weights, row_cell, col_cell, row_offset, col_offset,
    b_out, margin_out, one, two,
    ext, across, waves, mix, twist, last, first, turned_back, unmix,
    pick, col_taps_all, row_taps_all, table_hi, table_lo, values_hi, values_lo,
    parts, near, summed, far, mine, gathered, block, blocks, rim_row, rims,
    pack, left, right,
    g, edge, near2, near_edge, summed2, summed_edge, far2, far_edge, mine2, mine_edge,
    gathered2, edges, block2, blocks2, margin, margins,
    load_sem, near_sem, far_sem, plane_sem, depth_sem, local_sem, rim_sem, halo_sem,
    near_sem2, far_sem2, plane_sem2, depth_sem2, local_sem2, near_edge_sem, far_edge_sem,
    edge_sem, margin_sem,
):
    links = Links()
    v, z, w, f = links.v, links.z, links.w, links.f
    own = f * W + w
    vs = ((v + Z * W - 1) % (Z * W), v, (v + 1) % (Z * W))
    fs = ((f + F - 1) % F, f, (f + 1) % F)
    ring = [(vs[i], fs[k]) for i in range(3) for k in range(3) if (i, k) != (1, 1)]
    gathered_in = links.greet(ring)

    loads = []

    def load(src, dst):
        loads.append(pltpu.make_async_copy(src, dst, load_sem.at[len(loads)]))
        loads[-1].start()
        return loads[-1]

    span = COLS // CHUNKS
    wave_load = load(waves_all.at[v], waves)
    chunk_loads = [
        load(
            image.at[:, pl.ds(c * span, span)],
            ext.at[pl.ds(8, BAND), pl.ds(128 + c * span, span)],
        )
        for c in range(CHUNKS)
    ]
    forward_loads = [
        load(mix_all.at[w], mix), load(twist_all.at[own], twist), load(last_hbm, last),
    ]
    backward_loads = [
        load(first_hbm, first), load(turn_hbm, turned_back), load(unmix_all.at[own], unmix),
    ]

    o_of = lax.broadcasted_iota(jnp.int32, (16, 256), 1) // 16
    s_of = lax.broadcasted_iota(jnp.int32, (16, 256), 1) % 16
    rep = (lax.broadcasted_iota(jnp.int32, (16, 256), 0) == o_of).astype(f32)
    fanned = dot(kernel_t[...], rep, HI)
    padded = jnp.concatenate([fanned, jnp.zeros((8, 256), f32)], axis=0)
    tap_table = jnp.where(s_of == 0, padded, 0.0)
    for s in range(1, 9):
        tap_table = jnp.where(s_of == s, pltpu.roll(padded, s, 0), tap_table)
    tap_hi, tap_lo = split(tap_table)
    tap_both = jnp.concatenate([tap_hi, tap_lo], axis=0)
    down = lax.broadcasted_iota(jnp.int32, (256, 256), 0)
    first_col = f * COLS

    def onehot(index):
        return jnp.where(down == index, 1.0, 0.0).astype(bf16)

    def choose(step):
        lanes = pl.ds(pl.multiple_of(step * 256, 256), 256)
        col = col_cell[:, lanes] - first_col
        q = col // 8
        pick[:, lanes] = onehot((q % 8) * 32 + q // 8)
        col_taps = dot(tap_both, onehot(col_offset[:, lanes] * 16 + col % 8))
        col_taps_all[:, lanes] = col_taps[:16] + col_taps[16:]
        row_taps = dot(tap_both, onehot(row_offset[:, lanes] * 16 + row_cell[:, lanes]))
        row_taps_all[:, lanes] = row_taps[:16] + row_taps[16:]

    wave_load.wait()
    wave_hi, wave_lo = split(waves[...])
    both = jnp.concatenate([wave_hi, wave_lo], axis=0)
    for tile in range(8):
        if tile % (8 // CHUNKS) == 0:
            chunk_loads[tile // (8 // CHUNKS)].wait()
        hi, lo = split(ext[8 : 8 + BAND, 128 + tile * 256 : 384 + tile * 256])
        value = dot(both, hi)
        value = value[:32] + value[32:] + dot(wave_hi, lo)
        for half in range(2):
            c = (tile % 2) * 2 + half
            for im in range(2):
                parts[pl.ds((tile // 2) * 128 + im * 4 + c, 16, stride=8), :] = value[
                    im * 16 : im * 16 + 16, half * 128 : half * 128 + 128
                ]
    pack[0] = jnp.transpose(ext[8 : 8 + BAND, 128:256])[0:8]
    pack[1] = jnp.transpose(ext[8 : 8 + BAND, COLS : COLS + 128])[120:128]
    gathered_in()
    forward, result = links.reduce_rows(parts, near, near_sem, summed, far, far_sem)
    halo = []

    def halo_copy(src, dst, peer):
        halo.append(links.copy(src, dst, halo_sem, len(halo), peer))
        halo[-1].start()

    middle = pl.ds(128, COLS)
    halo_copy(ext.at[pl.ds(8, 8), middle], ext.at[pl.ds(BAND + 8, 8), middle], (vs[0], fs[1]))
    halo_copy(ext.at[pl.ds(BAND, 8), middle], ext.at[pl.ds(0, 8), middle], (vs[2], fs[1]))
    halo_copy(pack.at[0], right.at[:, pl.ds(128, 256)], (vs[1], fs[0]))
    halo_copy(pack.at[1], left.at[:, pl.ds(128, 256)], (vs[1], fs[2]))
    halo_copy(pack.at[0, :, pl.ds(0, 128)], right.at[:, pl.ds(384, 128)], (vs[0], fs[0]))
    halo_copy(pack.at[0, :, pl.ds(128, 128)], right.at[:, pl.ds(0, 128)], (vs[2], fs[0]))
    halo_copy(pack.at[1, :, pl.ds(0, 128)], left.at[:, pl.ds(384, 128)], (vs[0], fs[2]))
    halo_copy(pack.at[1, :, pl.ds(128, 128)], left.at[:, pl.ds(0, 128)], (vs[2], fs[2]))
    forward()

    low_row = jnp.where(v == 0, 8, 0)
    high_row = jnp.where(v == Z * W - 1, BAND + 8, TALL)
    low_col = jnp.where(f == 0, 128, 0)
    high_col = jnp.where(f == F - 1, COLS + 128, EXT)
    tall = lax.broadcasted_iota(jnp.int32, (TALL, 128), 0)
    rows_in = (tall >= low_row) & (tall < high_row)

    def assemble():
        for copy in halo:
            copy.wait()
        ext[0:8, middle] = jnp.where(low_row == 0, ext[0:8, middle], 0.0)
        bottom = pl.ds(BAND + 8, 8)
        ext[bottom, middle] = jnp.where(high_row == TALL, ext[bottom, middle], 0.0)
        side = jnp.concatenate([jnp.zeros((120, 512), f32), left[...]], axis=0)
        side = jnp.transpose(side)[120 : 120 + TALL]
        ext[:, 0:128] = jnp.where(rows_in & (low_col == 0), side, 0.0)
        side = jnp.concatenate([right[...], jnp.zeros((120, 512), f32)], axis=0)
        side = jnp.transpose(side)[120 : 120 + TALL]
        ext[:, EXT - 128 : EXT] = jnp.where(rows_in & (high_col == EXT), side, 0.0)

    def along_columns(dilation):
        def step(i):
            rows = pl.ds(pl.multiple_of(i * 8, 8), 8)
            across[rows, :] = weigh(ext[rows, :], dilation, 1)

        loop(TALL // 8, step)

    def smoothed_rows(i, dilation):
        lanes = pl.ds(pl.multiple_of(i * 128, 128), 128)
        return lanes, weigh(across[:, lanes], dilation, 0)

    def first_rows(i):
        lanes, value = smoothed_rows(i, 1)
        col = lax.broadcasted_iota(jnp.int32, (TALL, 128), 1) + i * 128
        value = jnp.where(rows_in & (col >= low_col) & (col < high_col), value, 0.0)
        ext[:, lanes] = value
        return value

    def keep_first(i):
        value = first_rows(i + 1)
        one[:, pl.ds(pl.multiple_of(i * 128, 128), 128)] = value[8 : 8 + BAND]

    def keep_second(i):
        lanes, value = smoothed_rows(i + 1, 2)
        two[:, pl.ds(pl.multiple_of(i * 128, 128), 128)] = value[8 : 8 + BAND]

    assemble()
    along_columns(1)
    total = result()
    mine[...] = total
    plane_wait = links.share_plane(mine, gathered, plane_sem)
    loop(VDEV // 256, choose)
    for copy in forward_loads:
        copy.wait()
    plane_wait()

    wide = jnp.concatenate(
        [gathered[pl.ds(0, 128, stride=2), :], gathered[pl.ds(1, 128, stride=2), :]], axis=1
    )
    mixed = dot(mix[...], wide, HI)
    cos, sin = twist[0], twist[1]
    turned_a, turned_b = [], []
    for part in range(5):
        size = 16 if part == 4 else 8
        a = mixed[part * 16 : part * 16 + size]
        b = mixed[part * 16 + size : part * 16 + 2 * size]
        c = cos[part * 8 : part * 8 + size]
        s = sin[part * 8 : part * 8 + size]
        turned_a.append(a * c + b * s)
        turned_b.append(b * c - a * s)
    turned = jnp.concatenate(
        [jnp.concatenate(turned_a, axis=0), jnp.concatenate(turned_b, axis=0)], axis=1
    )
    spec = dot(turned, last[...], HI)
    group8 = lax.broadcasted_iota(jnp.int32, (8, 128), 1) // 32
    value = spec[0:8]
    for b_lo in range(1, 4):
        value = jnp.where(group8 == b_lo, spec[b_lo * 8 : b_lo * 8 + 8], value)
    block[...] = value
    relay = links.spread(block, blocks, depth_sem, local_sem)
    diagonal = lax.broadcasted_iota(jnp.int32, (16, 128), 0) == lax.broadcasted_iota(
        jnp.int32, (16, 128), 1
    )
    corner = jnp.where(diagonal, jnp.broadcast_to(spec[32:48, 0:1], (16, 128)), 0.0)
    rim_row[...] = jnp.sum(corner, axis=0, keepdims=True)
    rim_wait = links.each_depth(lambda d: rim_row, lambda d: rims.at[z], rim_sem)
    rims[z] = rim_row[...]
    first_rows(0)
    loop(COLS // 128, keep_first)
    first_rows(EXT // 128 - 1)
    relay()
    rim_wait()

    lane = lax.broadcasted_iota(jnp.int32, (32, 256), 1)
    rim = jnp.concatenate([rims[r] for r in range(16)], axis=0)
    for j in range(8):
        both = []
        for im in range(2):
            halves = [
                blocks[pl.ds((j // 2) * 128 + im * 4 + (j % 2) * 2 + h, 16, stride=8), :]
                for h in range(2)
            ]
            both.append(jnp.concatenate(halves, axis=1))
        tile = jnp.concatenate(both, axis=0)
        hi, lo = split(tile)
        table_hi[j * 32 : j * 32 + 32, :] = hi
        table_lo[j * 32 : j * 32 + 32, :] = lo
        if j < 7:
            beyond = jnp.concatenate(
                [
                    jnp.broadcast_to(rim[:, im * 8 + j : im * 8 + j + 1], (16, 256))
                    for im in range(2)
                ],
                axis=0,
            )
            once = pltpu.roll(tile, 224, 1)
            twice = pltpu.roll(once, 255, 1)
            moved = jnp.where(lane < 224, once, jnp.where(lane == 255, beyond, twice))
            hi, lo = split(moved)
            table_hi[(j + 8) * 32 : (j + 9) * 32, :] = hi
            table_lo[(j + 8) * 32 : (j + 9) * 32, :] = lo

    def visit(step):
        lanes = pl.ds(pl.multiple_of(step * 256, 256), 256)
        chosen = pick[:, lanes]
        col_taps = col_taps_all[:, lanes]
        row_taps = row_taps_all[:, lanes]
        picked = dot(table_hi[...], chosen) + dot(table_lo[...], chosen)
        folded = picked[0:32] * col_taps[0:1]
        for d in range(1, TAPS):
            folded = folded + picked[d * 32 : d * 32 + 32] * col_taps[d : d + 1]
        misfit = []
        for im in range(2):
            model = jnp.sum(folded[im * 16 : im * 16 + 16] * row_taps, axis=0, keepdims=True)
            misfit.append(
                row_taps * (weights[:, lanes] * (model - observed[im : im + 1, lanes]))
            )
        fan = jnp.concatenate(misfit, axis=0)
        for d in range(TAPS):
            hi, lo = split(fan * col_taps[d : d + 1])
            values_hi[d * 32 : d * 32 + 32, lanes] = hi
            values_lo[d * 32 : d * 32 + 32, lanes] = lo

    loop(VDEV // 256, visit)

    def scatter(values):
        return lax.dot_general(
            values[...], pick[...], (((1,), (1,)), ((), ())), preferred_element_type=f32
        )

    grid = scatter(values_hi) + scatter(values_lo)
    lane_half = lax.broadcasted_iota(jnp.int32, (16, 128), 1)
    over_edge = [jnp.zeros((16, 128), f32)]
    for j in range(8):
        tile = grid[j * 32 : j * 32 + 32]
        if j < 7:
            over = grid[(j + 8) * 32 : (j + 9) * 32]
            once = pltpu.roll(over, 32, 1)
            twice = pltpu.roll(once, 1, 1)
            tile = tile + jnp.where(lane >= 32, once, jnp.where(lane == 0, 0.0, twice))
            for im in range(2):
                end = over[im * 16 : im * 16 + 16, 255:256]
                over_edge.append(
                    jnp.where(lane_half == im * 8 + j, jnp.broadcast_to(end, (16, 128)), 0.0)
                )
        for im in range(2):
            for h in range(2):
                g[pl.ds((j // 2) * 128 + im * 4 + (j % 2) * 2 + h, 16, stride=8), :] = tile[
                    im * 16 : im * 16 + 16, h * 128 : h * 128 + 128
                ]
    edge[...] = functools.reduce(jnp.add, over_edge)

    forward, result = links.reduce_rows(g, near2, near_sem2, summed2, far2, far_sem2)
    near_edges = [
        links.copy(edge, near_edge.at[d - 1], near_edge_sem, d, links.local(d))
        for d in range(1, W)
    ]
    for copy in near_edges:
        copy.start()
    forward()
    for copy in near_edges:
        copy.wait_recv()
        links.later(copy.wait_send)
    edge_sum = edge[...] + near_edge[0] + near_edge[1] + near_edge[2]
    for r in range(16):
        summed_edge[r] = edge_sum[r : r + 1]
    edge_wait = links.each_depth(
        lambda d: summed_edge.at[(z + d) % Z], lambda d: far_edge.at[d], far_edge_sem
    )
    along_columns(2)
    total = result()
    mine2[...] = total
    plane_wait = links.share_plane(mine2, gathered2, plane_sem2)
    edge_wait()
    edge_total = summed_edge[z]
    for d in range(1, Z):
        edge_total = edge_total + far_edge[d]
    mine_edge[...] = edge_total
    edge_copies = [
        links.copy(mine_edge, edges.at[f], edge_sem, df, links.plane(df, 0))
        for df in FACETS_FAR_FIRST[:-1]
    ]
    for copy in edge_copies:
        copy.start()
        links.later(copy.wait_send)
    edges[f] = edge_total
    loop(8, keep_second)
    for copy in backward_loads:
        copy.wait()
    for copy in edge_copies:
        copy.wait_recv()
    plane_wait()

    row_index = lax.broadcasted_iota(jnp.int32, (32, 128), 0)
    lane = lax.broadcasted_iota(jnp.int32, (32, 128), 1)
    target = ((row_index // 4) % 2) * 8 + 2 * (row_index // 8) + (row_index // 2) % 2
    wanted = (lane == target) & (row_index % 2 == 0)
    tiles = []
    for facet in range(F):
        tile = gathered2[facet * 32 : facet * 32 + 32]
        if facet:
            spill = jnp.where(wanted, jnp.broadcast_to(edges[facet - 1], (32, 128)), 0.0)
            column = jnp.sum(spill, axis=1, keepdims=True)
            tile = tile + jnp.where(lane == 0, jnp.broadcast_to(column, (32, 128)), 0.0)
        tiles.append(tile)
    group = lane // 32
    moved = [
        [tile if s == 0 else pltpu.roll(tile, 32 * s, 1) for s in range(4)] for tile in tiles
    ]
    rows = []
    for b_lo in range(4):
        halves = []
        for half in range(2):
            value = moved[half * 4][(0 - b_lo) % 4]
            for k in range(1, 4):
                value = jnp.where(group == k, moved[half * 4 + k][(k - b_lo) % 4], value)
            halves.append(value)
        rows.append(jnp.concatenate(halves, axis=1))
    stack = jnp.concatenate(rows, axis=0)
    sign = jnp.where(lax.broadcasted_iota(jnp.int32, (8, 256), 0) < 4, -1.0, 1.0)
    operand = jnp.concatenate([stack, rotate(stack, sign)], axis=1)
    spun = dot(operand, first[...], HI)
    spun = spun * turned_back[0] + rotate(spun, sign) * turned_back[1]
    out = dot(unmix[...], spun, HI)
    upper = lax.broadcasted_iota(jnp.int32, (8, 128), 0) < 4
    block2[...] = jnp.where(upper, out[0:8, 0:128], out[0:8, 128:256])
    relay = links.spread(block2, blocks2, depth_sem2, local_sem2)
    low = lax.broadcasted_iota(jnp.int32, (8, 128), 1) < 64
    sides = jnp.where(low, out[8:16, 0:128], out[16:24, 128:256])
    margin[...] = sides[0:2]
    margin_wait = links.each_depth(lambda d: margin, lambda d: margins.at[z], margin_sem)
    margins[z] = margin[...]
    loop(8, lambda i: keep_second(i + 8))
    relay()
    margin_wait()
    for r in range(16):
        for im in range(2):
            margin_out[im * 16 + r : im * 16 + r + 1, :] = margins[r, im : im + 1, :]
    b_out[...] = blocks2[...]
    links.finish()


def rotate(x, sign):
    groups = x.shape[0] // 8
    out = []
    for g in range(groups):
        out.append(pltpu.roll(x[g * 8 : g * 8 + 8], 4, 0) * sign)
    return jnp.concatenate(out, axis=0)


def weigh(x, dilation, axis):
    n = x.shape[axis]
    near = pltpu.roll(x, dilation, axis) + pltpu.roll(x, n - dilation, axis)
    wide = pltpu.roll(x, 2 * dilation, axis) + pltpu.roll(x, n - 2 * dilation, axis)
    return SPLINE[2] * x + (SPLINE[1] * near + SPLINE[0] * wide)


EXT = COLS + 256
TALL = BAND + 16


def final_kernel(image, one, two, b, margin, phase, waves, thresholds, out):
    v = lax.axis_index("vis")
    f = lax.axis_index("facet")
    edge = jnp.where(v == 0, 0, jnp.where(v == Z * W - 1, 2, 1))
    parts = []
    for im in range(2):
        tiles = [margin[im * 16 : im * 16 + 16, :]]
        for tile in range(16):
            w, l1, mh = tile // 4, (tile // 2) % 2, tile % 2
            tiles.append(b[pl.ds(w * 128 + mh * 4 + im * 2 + l1, 16, stride=8), :])
        tiles.append(margin[im * 16 : im * 16 + 16, :])
        parts.append(jnp.concatenate(tiles, axis=1))
    cos, sin = phase[0:16, 0:1], phase[16:32, 0:1]
    col = lax.broadcasted_iota(jnp.int32, (32, EXT), 1)
    low_col = jnp.where(f == 0, 128, 122)
    high_col = jnp.where(f == F - 1, COLS + 128, COLS + 134)
    inside = (col >= low_col) & (col < high_col)
    back = jnp.concatenate(
        [parts[0] * cos - parts[1] * sin, parts[1] * cos + parts[0] * sin], axis=0
    )
    levels = [jnp.where(inside, back, 0.0)]
    for dilation in (1, 2):
        levels.append(jnp.where(inside, weigh(levels[-1], dilation, 1), 0.0))
    operands = []
    for value in levels:
        hi, lo = split(value[:, 128 : 128 + COLS])
        operands.append(jnp.concatenate([hi, lo, hi], axis=0))
    for tile in range(COLS // 256):
        lanes = slice(tile * 256, tile * 256 + 256)
        c0 = image[:, lanes] - dot(waves[edge, 0], operands[0][:, lanes])
        c1 = one[:, lanes] - dot(waves[edge, 1], operands[1][:, lanes])
        c2 = two[:, lanes] - dot(waves[edge, 2], operands[2][:, lanes])
        d0, d1 = c0 - c1, c1 - c2
        t0, t1 = thresholds[0], thresholds[1]
        kept = (d0 - jnp.clip(d0, -t0, t0)) + (d1 - jnp.clip(d1, -t1, t1))
        out[:, lanes] = jnp.maximum(kept + c2, 0.0)


def vmem(count):
    return [pl.BlockSpec(memory_space=pltpu.VMEM)] * count


def anywhere(count):
    return [pl.BlockSpec(memory_space=pl.ANY)] * count


def sds(*shape, dtype=f32):
    return jax.ShapeDtypeStruct(shape, dtype)


LIMIT = 48 * 1024 * 1024


def pairs(count):
    return pltpu.SemaphoreType.DMA((2, count))


def on_device(
    image, observed, weights, row_cell, col_cell, row_offset, col_offset, kernel, thresholds
):
    root = math.sqrt(NPIX)
    scale = STEP * NPIX / (4.0 * math.sqrt(VDEV * Z * W * F)) / root / root
    V = pltpu.VMEM

    def row_buffers():
        return [V((384, 128), f32), V((128, 128), f32), V((128, 128), f32), V((8, 128), f32),
                V((256, 128), f32), V((8, 128), f32), V((512, 128), f32)]

    b, margin, one, two = pl.pallas_call(
        main_kernel,
        out_shape=[sds(512, 128), sds(32, 128), sds(BAND, COLS), sds(BAND, COLS)],
        in_specs=anywhere(8) + vmem(7),
        out_specs=vmem(4),
        scratch_shapes=[
            V((TALL, EXT), f32), V((TALL, EXT), f32),
            V((32, 256), f32), V((96, 128), f32), V((2, 48, 256), f32), V((512, 128), f32),
            V((512, 256), f32), V((2, 128, 256), f32), V((24, 128), f32),
            V((256, VDEV), bf16), V((16, VDEV), f32), V((16, VDEV), f32),
            V((480, 256), bf16), V((480, 256), bf16), V((480, VDEV), bf16),
            V((480, VDEV), bf16),
            V((512, 128), f32), V((384, 128), f32), V((128, 128), f32), V((128, 128), f32),
            V((8, 128), f32), V((256, 128), f32), V((8, 128), f32), V((512, 128), f32),
            V((1, 128), f32), V((16, 1, 128), f32),
            V((2, 8, 256), f32), V((8, 512), f32), V((8, 512), f32),
            V((512, 128), f32), V((16, 128), f32), V((384, 128), f32), V((3, 16, 128), f32),
            V((128, 128), f32), V((16, 1, 128), f32), V((128, 128), f32),
            V((16, 1, 128), f32), V((8, 128), f32), V((1, 128), f32),
            V((256, 128), f32), V((8, 1, 128), f32), V((8, 128), f32), V((512, 128), f32),
            V((2, 128), f32), V((16, 2, 128), f32),
            pltpu.SemaphoreType.DMA((16,)),
            pairs(48), pairs(16), pairs(32), pairs(16), pairs(48), pairs(16), pairs(8),
            pairs(48), pairs(16), pairs(32), pairs(16), pairs(48), pairs(4), pairs(16),
            pairs(8), pairs(16),
        ],
        compiler_params=pltpu.CompilerParams(
            vmem_limit_bytes=LIMIT, collective_id=0, has_side_effects=True
        ),
    )(
        image, jnp.asarray(band_waves()), jnp.asarray(forward_mix()),
        jnp.asarray(forward_twist()), jnp.asarray(forward_last() / 128.0),
        jnp.asarray(backward_first()), jnp.asarray(backward_twist()),
        jnp.asarray(backward_mix(scale)),
        kernel.T, observed, weights[None], row_cell[None], col_cell[None],
        row_offset[None], col_offset[None],
    )
    v = lax.axis_index("vis")
    phase = lax.dynamic_index_in_dim(jnp.asarray(band_phases()), v, 0, False)
    return pl.pallas_call(
        final_kernel,
        out_shape=sds(BAND, COLS),
        in_specs=vmem(7) + [pl.BlockSpec(memory_space=pltpu.SMEM)],
        out_specs=pl.BlockSpec(memory_space=pltpu.VMEM),
        compiler_params=pltpu.CompilerParams(vmem_limit_bytes=LIMIT),
    )(image, one, two, b, margin, phase, jnp.asarray(gradient_tables()), thresholds)


def solution(mesh):
    return jax.shard_map(
        on_device,
        mesh=mesh,
        in_specs=(
            P("vis", "facet"),
            P(None, ("vis", "facet")),
            P(("vis", "facet")),
            P(("vis", "facet")),
            P(("vis", "facet")),
            P(("vis", "facet")),
            P(("vis", "facet")),
            P(),
            P(),
        ),
        out_specs=P("vis", "facet"),
        check_vma=False,
    )
```

time: 126 us -> 104 us (0.83)
  Pallas kernels: 119 us -> 91.7 us
  local copies, waits for them, and re-layouts: 4.91 us -> 11.8 us
  other arithmetic: 1.35 us -> 0 us
    pallas_call x5 -> x2, Pallas kernels: 119 us -> 91.7 us  [the longest x1 86.8 us: on_device(): pl.pallas_call(main_kernel, out_shape=[sds(512, 128), sds(32, 128), sds(B...]
    unnamed x34 -> x32, local copies, waits for them, and re-layouts: 4.84 us -> 11.1 us
where the time goes in v2:
time: 104 us
  Pallas kernels  91.7 us (88%)
  local copies, waits for them, and re-layouts  11.8 us (11%)
    pallas_call x1, Pallas kernels, on_device(): pl.pallas_call(main_kernel, out_shape=[sds(512, 128), sds(32, 128), sds(B...  86.8 us
    unnamed x32, local copies, waits for them, and re-layouts  11.1 us
    pallas_call x1, Pallas kernels, on_device(): pl.pallas_call(final_kernel, out_shape=sds(BAND, COLS), in_specs=vmem(7)...  4.97 us

profile of v2, /device:TPU:1, one launch (start us, length us, event | category | flops | bytes accessed | tf_op | source)
XLA Modules:
  0.0 103.6 jit_solution(17912000573529193066)
XLA Ops:
  0.0 0.7 dynamic-slice_bitcast_fusion.phase
  0.7 0.0 copy-start.3
  0.7 1.0 %copy-done.3 = f32[512,256]{1,0:T(8,128)S(1)} copy-done((f32[512,256]{1,0:T(8,128)S(1)}, f32[512,256]{1,0:T(8,128)}, u32[]{:S(2)}) %copy-start.3) | copy-done | bytes 524312
  1.8 0.0 copy-start.4
  1.8 1.0 copy-done.4
  2.8 0.0 copy-start.5
  2.8 0.9 copy-done.5
  3.7 0.0 copy-start.6
  3.7 0.9 copy-done.6
  4.7 0.9 copy-done.7
  5.6 0.7 copy-done.8
  6.3 0.7 copy-done.9
  7.0 0.7 copy-done.10
  7.7 0.7 copy-done.11
  8.4 0.7 copy-done.12
  9.1 0.7 copy-done.13
  9.8 0.7 copy-done.14
  10.5 86.8 %shard_map.172 = (f32[512,128]{1,0:T(8,128)S(1)}, f32[32,128]{1,0:T(8,128)S(1)}, f32[256,2048]{1,0:T(8,128)S(1)}, f32[256,2048]{1,0:T(8,128)S(1)}) custom-call(f32[256,2048]{1,0:T(8,128)} %image.3, f32[64,32,256]{2,1,0:T(8,128)} %constant.30.clone.waves_all, f32[4,96,128]{2,1,0:T(8,128)S(1)} %copy-done.7, f32[32,2,48,256]{3,2,1,0:T(8,128)} %constant.32.clone.twist_all, ...), custom_call_target="tpu_custom_call" | custom-call | tf_op jit(solution)/shard_map/pallas_call | solution.py:856
  97.3 0.0 copy-start.1
  97.3 1.3 %copy-done.1 = f32[256,2048]{1,0:T(8,128)} copy-done((f32[256,2048]{1,0:T(8,128)}, f32[256,2048]{1,0:T(8,128)S(1)}, u32[]{:S(2)}) %copy-start.1) | copy-done | bytes 2097176
  98.6 0.0 copy-done
  98.6 0.0 copy-done.2
  98.6 0.0 copy-done.15
  98.6 5.0 %shard_map.173 = f32[256,2048]{1,0:T(8,128)} custom-call(f32[256,2048]{1,0:T(8,128)S(1)} %copy-done, f32[256,2048]{1,0:T(8,128)S(1)} %get-tuple-element.9.one, f32[256,2048]{1,0:T(8,128)} %copy-done.1, f32[512,128]{1,0:T(8,128)S(1)} %get-tuple-element.11.b, f32[32,128]{1,0:T(8,128)S(1)} %get-tuple-element.12.margin, ...), custom_call_target="tpu_custom_call" | custom-call | tf_op jit(solution)/shard_map/pallas_call | solution.py:895
  (11 shorter events, 0.0 us)
Async XLA Ops:
  0.7 1.0 %copy-start.3 = (f32[512,256]{1,0:T(8,128)S(1)}, f32[512,256]{1,0:T(8,128)}, u32[]{:S(2)}) copy-start(f32[512,256]{1,0:T(8,128)} %constant.34.clone.first_hbm) | copy-start | bytes 1572868
  1.8 1.0 copy-start.4
  2.8 0.9 copy-start.5
  3.7 0.9 copy-start.6
  4.7 0.9 copy-start.7
  5.6 0.7 copy-start.8
  6.3 0.7 copy-start.9
  7.0 0.7 copy-start.10
  7.7 0.7 copy-start.11
  8.4 0.7 copy-start.12
  9.1 0.7 copy-start.13
  9.8 0.7 copy-start.14
  10.5 88.1 %copy-start = (f32[256,2048]{1,0:T(8,128)S(1)}, f32[256,2048]{1,0:T(8,128)}, u32[]{:S(2)}) copy-start(f32[256,2048]{1,0:T(8,128)} %image.3) | copy-start | bytes 6291460
  10.5 88.1 %copy-start.2 = (bf16[3,3,256,96]{3,2,1,0:T(8,128)(2,1)S(1)}, bf16[3,3,256,96]{3,2,1,0:T(8,128)(2,1)}, u32[]{:S(2)}) copy-start(bf16[3,3,256,96]{3,2,1,0:T(8,128)(2,1)} %constant.38.clone.waves) | copy-start | bytes 1327108
  10.5 88.1 %copy-start.15 = (f32[2]{0:T(128)S(1)}, f32[2]{0:T(128)}, u32[]{:S(2)}) copy-start(f32[2]{0:T(128)} %thresholds.1) | copy-start | bytes 28
  97.3 1.3 %copy-start.1 = (f32[256,2048]{1,0:T(8,128)}, f32[256,2048]{1,0:T(8,128)S(1)}, u32[]{:S(2)}) copy-start(f32[256,2048]{1,0:T(8,128)S(1)} %get-tuple-element.10.two) | copy-start | bytes 6291460

commit v3 on v2

--- a/solution.py
+++ b/solution.py
@@ -238,11 +238,14 @@
     def plane(self, df, dw):
         return (self.z * W + (self.w + dw) % W, (self.f + df) % F)
 
-    def copy(self, src, dst, sems, slot, peer):
+    def copy(self, src, dst, send, recv, peer):
         return pltpu.make_async_remote_copy(
-            src_ref=src, dst_ref=dst, send_sem=sems.at[0, slot], recv_sem=sems.at[1, slot],
+            src_ref=src, dst_ref=dst, send_sem=send, recv_sem=recv,
             device_id=peer, device_id_type=MESH,
         )
+
+    def bytes_of(self, ref, sem):
+        return self.copy(ref, ref, sem, sem, self.depth(1))
 
     def greet(self, extra):
         barrier = pltpu.get_barrier_semaphore()
@@ -267,29 +270,20 @@
             wait()
 
     def reduce_rows(self, parts, near, near_sem, summed, far, far_sem):
-        def near_copy(row, d):
-            here = ((self.w + d) % W) * Z + row
-            return self.copy(
-                rows8(parts, here), rows8(near, (d - 1) * Z + row), near_sem,
-                (d - 1) * Z + row, self.local(d),
-            )
-
-        def far_copy(d):
-            row = (self.z + d) % Z
-            return self.copy(rows8(summed, row), rows8(far, d), far_sem, d, self.depth(d))
-
         def send_row(row):
             for d in range(1, W):
-                near_copy(row, d).start()
+                here = ((self.w + d) % W) * Z + row
+                self.copy(
+                    rows8(parts, here), rows8(near, row * (W - 1) + d - 1), near_sem.at[Z],
+                    near_sem.at[row], self.local(d),
+                ).start()
 
         def sum_row(row):
-            for d in range(1, W):
-                near_copy(row, d).wait_recv()
+            start = pl.multiple_of(row * (8 * (W - 1)), 8)
+            self.bytes_of(near.at[pl.ds(start, 8 * (W - 1))], near_sem.at[row]).wait_recv()
             value = parts[pl.ds(pl.multiple_of((self.w * Z + row) * 8, 8), 8), :]
-            for d in range(1, W):
-                value = value + near[
-                    pl.ds(pl.multiple_of(((d - 1) * Z + row) * 8, 8), 8), :
-                ]
+            for d in range(W - 1):
+                value = value + near[pl.ds(pl.multiple_of(start + d * 8, 8), 8), :]
             summed[pl.ds(pl.multiple_of(row * 8, 8), 8), :] = value
 
         loop(Z - 1, lambda i: send_row((self.z + far_first(i)) % Z))
@@ -298,68 +292,61 @@
         def forward():
             def step(i):
                 d = far_first(i)
-                sum_row((self.z + d) % Z)
-                far_copy(d).start()
+                row = (self.z + d) % Z
+                sum_row(row)
+                self.copy(
+                    rows8(summed, row), rows8(far, d - 1), far_sem.at[0], far_sem.at[1],
+                    self.depth(d),
+                ).start()
 
             loop(Z - 1, step)
             sum_row(self.z)
 
         def result():
-            loop(Z - 1, lambda i: far_copy(i + 1).wait_recv())
+            self.bytes_of(far, far_sem.at[1]).wait_recv()
             value = summed[pl.ds(pl.multiple_of(self.z * 8, 8), 8), :]
-            for d in range(1, Z):
+            for d in range(Z - 1):
                 value = value + far[d * 8 : d * 8 + 8]
             return value
 
-        def done(row):
-            for d in range(1, W):
-                near_copy(row, d).wait_send()
-
-        self.later(lambda: loop(Z, done))
-        self.later(lambda: loop(Z - 1, lambda i: far_copy(i + 1).wait_send()))
+        self.later(self.bytes_of(near, near_sem.at[Z]).wait_send)
+        self.later(self.bytes_of(far, far_sem.at[0]).wait_send)
         return forward, result
 
     def share_plane(self, mine, gathered, sem):
         own = self.f * W + self.w
-
-        def each(act):
-            for df in FACETS_FAR_FIRST:
-                first = 0 if df else 1
-                loop(
-                    W - first,
-                    lambda i: act(
-                        self.copy(
-                            mine, rows8(gathered, own), sem, df * W + i + first,
-                            self.plane(df, i + first),
-                        )
-                    ),
-                )
-
-        each(lambda c: c.start())
+        for df in FACETS_FAR_FIRST:
+            first = 0 if df else 1
+            loop(
+                W - first,
+                lambda i: self.copy(
+                    mine, rows8(gathered, own), sem.at[0], sem.at[1],
+                    self.plane(df, i + first),
+                ).start(),
+            )
         gathered[pl.ds(pl.multiple_of(own * 8, 8), 8), :] = mine[...]
-        self.later(lambda: each(lambda c: c.wait_send()))
-        return lambda: each(lambda c: c.wait_recv())
+        whole = gathered.at[pl.ds(0, 8 * (F * W - 1))]
+        self.later(self.bytes_of(whole, sem.at[0]).wait_send)
+        return self.bytes_of(whole, sem.at[1]).wait_recv
 
     def spread(self, block, blocks, depth_sem, local_sem):
         def depth_copy(d):
             return self.copy(
-                block, rows8(blocks, self.w * Z + self.z), depth_sem, d, self.depth(d)
+                block, rows8(blocks, self.w * Z + self.z), depth_sem.at[0], depth_sem.at[d],
+                self.depth(d),
             )
 
-        def local_copy(row, d):
-            slot = self.w * Z + row
-            return self.copy(
-                rows8(blocks, slot), rows8(blocks, slot), local_sem, (d - 1) * Z + row,
-                self.local(d),
-            )
-
         def pass_on(row):
+            slot = rows8(blocks, self.w * Z + row)
             for d in range(1, W):
-                local_copy(row, d).start()
+                self.copy(
+                    slot, slot, local_sem.at[0], local_sem.at[1], self.local(d)
+                ).start()
 
         loop(Z - 1, lambda i: depth_copy(far_first(i)).start())
         blocks[pl.ds(pl.multiple_of((self.w * Z + self.z) * 8, 8), 8), :] = block[...]
         pass_on(self.z)
+        others = blocks.at[pl.ds(0, 128 * (W - 1))]
 
         def relay():
             def step(i):
@@ -368,28 +355,21 @@
                 pass_on((self.z - d + Z) % Z)
 
             loop(Z - 1, step)
-
-            def arrived(row):
-                for d in range(1, W):
-                    local_copy(row, d).wait_recv()
-
-            loop(Z, arrived)
-
-        def done(row):
-            for d in range(1, W):
-                local_copy(row, d).wait_send()
-
-        self.later(lambda: loop(Z - 1, lambda i: depth_copy(i + 1).wait_send()))
-        self.later(lambda: loop(Z, done))
+            self.bytes_of(others, local_sem.at[1]).wait_recv()
+
+        self.later(self.bytes_of(blocks.at[pl.ds(0, 8 * (Z - 1))], depth_sem.at[0]).wait_send)
+        self.later(self.bytes_of(others, local_sem.at[0]).wait_send)
         return relay
 
-    def each_depth(self, src, dst, sem):
-        def make(d):
-            return self.copy(src(d), dst(d), sem, d, self.depth(d))
-
-        loop(Z - 1, lambda i: make(far_first(i)).start())
-        self.later(lambda: loop(Z - 1, lambda i: make(i + 1).wait_send()))
-        return lambda: loop(Z - 1, lambda i: make(i + 1).wait_recv())
+    def each_depth(self, src, dst, held, sem):
+        def send(i):
+            d = far_first(i)
+            self.copy(src(d), dst(d), sem.at[0], sem.at[1], self.depth(d)).start()
+
+        loop(Z - 1, send)
+        whole = held.at[pl.ds(0, Z - 1)]
+        self.later(self.bytes_of(whole, sem.at[0]).wait_send)
+        return self.bytes_of(whole, sem.at[1]).wait_recv
 
 
 EXT = COLS + 256
@@ -399,9 +379,11 @@
 
 def main_kernel(
     image, waves_all, mix_all, twist_all, last_hbm, first_hbm, turn_hbm, unmix_all,
+    phase_all, slopes_hbm, kernel_hbm, observed_hbm, weights_hbm, row_cell_hbm, col_cell_hbm, row_offset_hbm,
+    col_offset_hbm,
+    thresholds, out_hbm,
     kernel_t, observed, weights, row_cell, col_cell, row_offset, col_offset,
-    b_out, margin_out, one, two,
-    ext, across, waves, mix, twist, last, first, turned_back, unmix,
+    phase, slopes, out, one, two, ext, across, waves, mix, twist, last, first, turned_back, unmix,
     pick, col_taps_all, row_taps_all, table_hi, table_lo, values_hi, values_lo,
     parts, near, summed, far, mine, gathered, block, blocks, rim_row, rims,
     pack, left, right,
@@ -409,7 +391,7 @@
     gathered2, edges, block2, blocks2, margin, margins,
     load_sem, near_sem, far_sem, plane_sem, depth_sem, local_sem, rim_sem, halo_sem,
     near_sem2, far_sem2, plane_sem2, depth_sem2, local_sem2, near_edge_sem, far_edge_sem,
-    edge_sem, margin_sem,
+    edge_sem, margin_sem, store_sem,
 ):
     links = Links()
     v, z, w, f = links.v, links.z, links.w, links.f
@@ -427,6 +409,10 @@
         return loads[-1]
 
     span = COLS // CHUNKS
+    early_loads = [
+        load(kernel_hbm, kernel_t), load(row_cell_hbm, row_cell), load(col_cell_hbm, col_cell),
+        load(row_offset_hbm, row_offset), load(col_offset_hbm, col_offset),
+    ]
     wave_load = load(waves_all.at[v], waves)
     chunk_loads = [
         load(
@@ -436,12 +422,16 @@
         for c in range(CHUNKS)
     ]
     forward_loads = [
+        load(observed_hbm, observed), load(weights_hbm, weights),
         load(mix_all.at[w], mix), load(twist_all.at[own], twist), load(last_hbm, last),
     ]
     backward_loads = [
+        load(phase_all.at[v], phase), load(slopes_hbm, slopes),
         load(first_hbm, first), load(turn_hbm, turned_back), load(unmix_all.at[own], unmix),
     ]
 
+    for copy in early_loads:
+        copy.wait()
     o_of = lax.broadcasted_iota(jnp.int32, (16, 256), 1) // 16
     s_of = lax.broadcasted_iota(jnp.int32, (16, 256), 1) % 16
     rep = (lax.broadcasted_iota(jnp.int32, (16, 256), 0) == o_of).astype(f32)
@@ -490,7 +480,9 @@
     halo = []
 
     def halo_copy(src, dst, peer):
-        halo.append(links.copy(src, dst, halo_sem, len(halo), peer))
+        halo.append(
+            links.copy(src, dst, halo_sem.at[0, len(halo)], halo_sem.at[1, len(halo)], peer)
+        )
         halo[-1].start()
 
     middle = pl.ds(128, COLS)
@@ -524,7 +516,7 @@
         side = jnp.transpose(side)[120 : 120 + TALL]
         ext[:, EXT - 128 : EXT] = jnp.where(rows_in & (high_col == EXT), side, 0.0)
 
-    def along_columns(dilation):
+    def along_columns(ext, dilation):
         def step(i):
             rows = pl.ds(pl.multiple_of(i * 8, 8), 8)
             across[rows, :] = weigh(ext[rows, :], dilation, 1)
@@ -539,19 +531,14 @@
         lanes, value = smoothed_rows(i, 1)
         col = lax.broadcasted_iota(jnp.int32, (TALL, 128), 1) + i * 128
         value = jnp.where(rows_in & (col >= low_col) & (col < high_col), value, 0.0)
-        ext[:, lanes] = value
-        return value
-
-    def keep_first(i):
-        value = first_rows(i + 1)
-        one[:, pl.ds(pl.multiple_of(i * 128, 128), 128)] = value[8 : 8 + BAND]
+        one[:, lanes] = value
 
     def keep_second(i):
         lanes, value = smoothed_rows(i + 1, 2)
         two[:, pl.ds(pl.multiple_of(i * 128, 128), 128)] = value[8 : 8 + BAND]
 
     assemble()
-    along_columns(1)
+    along_columns(ext, 1)
     total = result()
     mine[...] = total
     plane_wait = links.share_plane(mine, gathered, plane_sem)
@@ -589,11 +576,9 @@
     )
     corner = jnp.where(diagonal, jnp.broadcast_to(spec[32:48, 0:1], (16, 128)), 0.0)
     rim_row[...] = jnp.sum(corner, axis=0, keepdims=True)
-    rim_wait = links.each_depth(lambda d: rim_row, lambda d: rims.at[z], rim_sem)
+    rim_wait = links.each_depth(lambda d: rim_row, lambda d: rims.at[z], rims, rim_sem)
     rims[z] = rim_row[...]
-    first_rows(0)
-    loop(COLS // 128, keep_first)
-    first_rows(EXT // 128 - 1)
+    loop(EXT // 128, first_rows)
     relay()
     rim_wait()
 
@@ -677,44 +662,39 @@
     edge[...] = functools.reduce(jnp.add, over_edge)
 
     forward, result = links.reduce_rows(g, near2, near_sem2, summed2, far2, far_sem2)
-    near_edges = [
-        links.copy(edge, near_edge.at[d - 1], near_edge_sem, d, links.local(d))
-        for d in range(1, W)
-    ]
-    for copy in near_edges:
-        copy.start()
+    for d in range(1, W):
+        links.copy(
+            edge, near_edge.at[d - 1], near_edge_sem.at[0], near_edge_sem.at[1], links.local(d)
+        ).start()
+    links.later(links.bytes_of(near_edge, near_edge_sem.at[0]).wait_send)
     forward()
-    for copy in near_edges:
-        copy.wait_recv()
-        links.later(copy.wait_send)
+    links.bytes_of(near_edge, near_edge_sem.at[1]).wait_recv()
     edge_sum = edge[...] + near_edge[0] + near_edge[1] + near_edge[2]
     for r in range(16):
         summed_edge[r] = edge_sum[r : r + 1]
     edge_wait = links.each_depth(
-        lambda d: summed_edge.at[(z + d) % Z], lambda d: far_edge.at[d], far_edge_sem
+        lambda d: summed_edge.at[(z + d) % Z], lambda d: far_edge.at[d - 1], far_edge,
+        far_edge_sem,
     )
-    along_columns(2)
+    along_columns(one, 2)
     total = result()
     mine2[...] = total
     plane_wait = links.share_plane(mine2, gathered2, plane_sem2)
     edge_wait()
     edge_total = summed_edge[z]
-    for d in range(1, Z):
+    for d in range(Z - 1):
         edge_total = edge_total + far_edge[d]
     mine_edge[...] = edge_total
-    edge_copies = [
-        links.copy(mine_edge, edges.at[f], edge_sem, df, links.plane(df, 0))
-        for df in FACETS_FAR_FIRST[:-1]
-    ]
-    for copy in edge_copies:
-        copy.start()
-        links.later(copy.wait_send)
+    for df in FACETS_FAR_FIRST[:-1]:
+        links.copy(
+            mine_edge, edges.at[f], edge_sem.at[0], edge_sem.at[1], links.plane(df, 0)
+        ).start()
+    links.later(links.bytes_of(edges.at[pl.ds(0, F - 1)], edge_sem.at[0]).wait_send)
     edges[f] = edge_total
     loop(8, keep_second)
     for copy in backward_loads:
         copy.wait()
-    for copy in edge_copies:
-        copy.wait_recv()
+    links.bytes_of(edges.at[pl.ds(0, F - 1)], edge_sem.at[1]).wait_recv()
     plane_wait()
 
     row_index = lax.broadcasted_iota(jnp.int32, (32, 128), 0)
@@ -747,61 +727,34 @@
     operand = jnp.concatenate([stack, rotate(stack, sign)], axis=1)
     spun = dot(operand, first[...], HI)
     spun = spun * turned_back[0] + rotate(spun, sign) * turned_back[1]
-    out = dot(unmix[...], spun, HI)
+    solved = dot(unmix[...], spun, HI)
     upper = lax.broadcasted_iota(jnp.int32, (8, 128), 0) < 4
-    block2[...] = jnp.where(upper, out[0:8, 0:128], out[0:8, 128:256])
+    block2[...] = jnp.where(upper, solved[0:8, 0:128], solved[0:8, 128:256])
     relay = links.spread(block2, blocks2, depth_sem2, local_sem2)
     low = lax.broadcasted_iota(jnp.int32, (8, 128), 1) < 64
-    sides = jnp.where(low, out[8:16, 0:128], out[16:24, 128:256])
+    sides = jnp.where(low, solved[8:16, 0:128], solved[16:24, 128:256])
     margin[...] = sides[0:2]
-    margin_wait = links.each_depth(lambda d: margin, lambda d: margins.at[z], margin_sem)
+    margin_wait = links.each_depth(lambda d: margin, lambda d: margins.at[z], margins, margin_sem)
     margins[z] = margin[...]
     loop(8, lambda i: keep_second(i + 8))
     relay()
     margin_wait()
-    for r in range(16):
-        for im in range(2):
-            margin_out[im * 16 + r : im * 16 + r + 1, :] = margins[r, im : im + 1, :]
-    b_out[...] = blocks2[...]
-    links.finish()
-
-
-def rotate(x, sign):
-    groups = x.shape[0] // 8
-    out = []
-    for g in range(groups):
-        out.append(pltpu.roll(x[g * 8 : g * 8 + 8], 4, 0) * sign)
-    return jnp.concatenate(out, axis=0)
-
-
-def weigh(x, dilation, axis):
-    n = x.shape[axis]
-    near = pltpu.roll(x, dilation, axis) + pltpu.roll(x, n - dilation, axis)
-    wide = pltpu.roll(x, 2 * dilation, axis) + pltpu.roll(x, n - 2 * dilation, axis)
-    return SPLINE[2] * x + (SPLINE[1] * near + SPLINE[0] * wide)
-
-
-EXT = COLS + 256
-TALL = BAND + 16
-
-
-def final_kernel(image, one, two, b, margin, phase, waves, thresholds, out):
-    v = lax.axis_index("vis")
-    f = lax.axis_index("facet")
-    edge = jnp.where(v == 0, 0, jnp.where(v == Z * W - 1, 2, 1))
+
+    variant = (v + Z * W - 1) // (Z * W) + (v + 1) // (Z * W)
     parts = []
     for im in range(2):
-        tiles = [margin[im * 16 : im * 16 + 16, :]]
+        rim = jnp.concatenate([margins[r, im : im + 1, :] for r in range(16)], axis=0)
+        tiles = [rim]
         for tile in range(16):
-            w, l1, mh = tile // 4, (tile // 2) % 2, tile % 2
-            tiles.append(b[pl.ds(w * 128 + mh * 4 + im * 2 + l1, 16, stride=8), :])
-        tiles.append(margin[im * 16 : im * 16 + 16, :])
+            start = (tile // 4) * 128 + (tile % 2) * 4 + im * 2 + (tile // 2) % 2
+            tiles.append(blocks2[pl.ds(start, 16, stride=8), :])
+        tiles.append(rim)
         parts.append(jnp.concatenate(tiles, axis=1))
     cos, sin = phase[0:16, 0:1], phase[16:32, 0:1]
     col = lax.broadcasted_iota(jnp.int32, (32, EXT), 1)
-    low_col = jnp.where(f == 0, 128, 122)
-    high_col = jnp.where(f == F - 1, COLS + 128, COLS + 134)
-    inside = (col >= low_col) & (col < high_col)
+    inside = (col >= jnp.where(f == 0, 128, 122)) & (
+        col < jnp.where(f == F - 1, COLS + 128, COLS + 134)
+    )
     back = jnp.concatenate(
         [parts[0] * cos - parts[1] * sin, parts[1] * cos + parts[0] * sin], axis=0
     )
@@ -812,34 +765,63 @@
     for value in levels:
         hi, lo = split(value[:, 128 : 128 + COLS])
         operands.append(jnp.concatenate([hi, lo, hi], axis=0))
+    t0, t1 = thresholds[0], thresholds[1]
+    stores = []
     for tile in range(COLS // 256):
         lanes = slice(tile * 256, tile * 256 + 256)
-        c0 = image[:, lanes] - dot(waves[edge, 0], operands[0][:, lanes])
-        c1 = one[:, lanes] - dot(waves[edge, 1], operands[1][:, lanes])
-        c2 = two[:, lanes] - dot(waves[edge, 2], operands[2][:, lanes])
+        held = slice(128 + tile * 256, 384 + tile * 256)
+        c0 = ext[8 : 8 + BAND, held] - dot(slopes[variant, 0], operands[0][:, lanes])
+        c1 = one[8 : 8 + BAND, held] - dot(slopes[variant, 1], operands[1][:, lanes])
+        c2 = two[:, lanes] - dot(slopes[variant, 2], operands[2][:, lanes])
         d0, d1 = c0 - c1, c1 - c2
-        t0, t1 = thresholds[0], thresholds[1]
         kept = (d0 - jnp.clip(d0, -t0, t0)) + (d1 - jnp.clip(d1, -t1, t1))
-        out[:, lanes] = jnp.maximum(kept + c2, 0.0)
-
-
-def vmem(count):
-    return [pl.BlockSpec(memory_space=pltpu.VMEM)] * count
+        out[:, lanes] = kept + c2
+        region = pl.ds(tile * 256, 256)
+        stores.append(
+            pltpu.make_async_copy(out.at[:, region], out_hbm.at[:, region], store_sem.at[tile])
+        )
+        stores[-1].start()
+    links.finish()
+    for copy in stores:
+        copy.wait()
+
+
+def rotate(x, sign):
+    groups = x.shape[0] // 8
+    out = []
+    for g in range(groups):
+        out.append(pltpu.roll(x[g * 8 : g * 8 + 8], 4, 0) * sign)
+    return jnp.concatenate(out, axis=0)
+
+
+def weigh(x, dilation, axis):
+    n = x.shape[axis]
+    near = pltpu.roll(x, dilation, axis) + pltpu.roll(x, n - dilation, axis)
+    wide = pltpu.roll(x, 2 * dilation, axis) + pltpu.roll(x, n - 2 * dilation, axis)
+    return SPLINE[2] * x + (SPLINE[1] * near + SPLINE[0] * wide)
+
+
+EXT = COLS + 256
+TALL = BAND + 16
 
 
 def anywhere(count):
-    return [pl.BlockSpec(memory_space=pl.ANY)] * count
+    return [pl.BlockSpec(memory_space=pltpu.HBM)] * count
 
 
 def sds(*shape, dtype=f32):
     return jax.ShapeDtypeStruct(shape, dtype)
 
 
-LIMIT = 48 * 1024 * 1024
+LIMIT = 60 * 1024 * 1024
 
 
 def pairs(count):
     return pltpu.SemaphoreType.DMA((2, count))
+
+
+def sems(count):
+    return pltpu.SemaphoreType.DMA((count,))
 
 
 def on_device(
@@ -849,35 +831,35 @@
     scale = STEP * NPIX / (4.0 * math.sqrt(VDEV * Z * W * F)) / root / root
     V = pltpu.VMEM
 
-    def row_buffers():
-        return [V((384, 128), f32), V((128, 128), f32), V((128, 128), f32), V((8, 128), f32),
-                V((256, 128), f32), V((8, 128), f32), V((512, 128), f32)]
-
-    b, margin, one, two = pl.pallas_call(
+    result = pl.pallas_call(
         main_kernel,
-        out_shape=[sds(512, 128), sds(32, 128), sds(BAND, COLS), sds(BAND, COLS)],
-        in_specs=anywhere(8) + vmem(7),
-        out_specs=vmem(4),
+        out_shape=sds(BAND, COLS),
+        in_specs=anywhere(17) + [pl.BlockSpec(memory_space=pltpu.SMEM)],
+        out_specs=pl.BlockSpec(memory_space=pltpu.HBM),
         scratch_shapes=[
-            V((TALL, EXT), f32), V((TALL, EXT), f32),
+            V((KW, ROWS), f32), V((2, VDEV), f32), V((1, VDEV), f32),
+            V((1, VDEV), jnp.int32), V((1, VDEV), jnp.int32), V((1, VDEV), jnp.int32),
+            V((1, VDEV), jnp.int32),
+            V((32, 128), f32), V((3, 3, BAND, 96), bf16), V((BAND, COLS), f32),
+            V((TALL, EXT), f32), V((BAND, COLS), f32), V((TALL, EXT), f32), V((TALL, EXT), f32),
             V((32, 256), f32), V((96, 128), f32), V((2, 48, 256), f32), V((512, 128), f32),
             V((512, 256), f32), V((2, 128, 256), f32), V((24, 128), f32),
             V((256, VDEV), bf16), V((16, VDEV), f32), V((16, VDEV), f32),
             V((480, 256), bf16), V((480, 256), bf16), V((480, VDEV), bf16),
             V((480, VDEV), bf16),
-            V((512, 128), f32), V((384, 128), f32), V((128, 128), f32), V((128, 128), f32),
+            V((512, 128), f32), V((384, 128), f32), V((128, 128), f32), V((120, 128), f32),
             V((8, 128), f32), V((256, 128), f32), V((8, 128), f32), V((512, 128), f32),
             V((1, 128), f32), V((16, 1, 128), f32),
             V((2, 8, 256), f32), V((8, 512), f32), V((8, 512), f32),
             V((512, 128), f32), V((16, 128), f32), V((384, 128), f32), V((3, 16, 128), f32),
-            V((128, 128), f32), V((16, 1, 128), f32), V((128, 128), f32),
-            V((16, 1, 128), f32), V((8, 128), f32), V((1, 128), f32),
+            V((128, 128), f32), V((16, 1, 128), f32), V((120, 128), f32),
+            V((15, 1, 128), f32), V((8, 128), f32), V((1, 128), f32),
             V((256, 128), f32), V((8, 1, 128), f32), V((8, 128), f32), V((512, 128), f32),
             V((2, 128), f32), V((16, 2, 128), f32),
-            pltpu.SemaphoreType.DMA((16,)),
-            pairs(48), pairs(16), pairs(32), pairs(16), pairs(48), pairs(16), pairs(8),
-            pairs(48), pairs(16), pairs(32), pairs(16), pairs(48), pairs(4), pairs(16),
-            pairs(8), pairs(16),
+            pltpu.SemaphoreType.DMA((24,)),
+            sems(17), sems(2), sems(2), sems(16), sems(2), sems(2), pairs(8),
+            sems(17), sems(2), sems(2), sems(16), sems(2), sems(2), sems(2), sems(2), sems(2),
+            sems(8),
         ],
         compiler_params=pltpu.CompilerParams(
             vmem_limit_bytes=LIMIT, collective_id=0, has_side_effects=True
@@ -886,19 +868,11 @@
         image, jnp.asarray(band_waves()), jnp.asarray(forward_mix()),
         jnp.asarray(forward_twist()), jnp.asarray(forward_last() / 128.0),
         jnp.asarray(backward_first()), jnp.asarray(backward_twist()),
-        jnp.asarray(backward_mix(scale)),
-        kernel.T, observed, weights[None], row_cell[None], col_cell[None],
-        row_offset[None], col_offset[None],
+        jnp.asarray(backward_mix(scale)), jnp.asarray(band_phases()),
+        jnp.asarray(gradient_tables()), kernel.T, observed, weights[None], row_cell[None],
+        col_cell[None], row_offset[None], col_offset[None], thresholds,
     )
-    v = lax.axis_index("vis")
-    phase = lax.dynamic_index_in_dim(jnp.asarray(band_phases()), v, 0, False)
-    return pl.pallas_call(
-        final_kernel,
-        out_shape=sds(BAND, COLS),
-        in_specs=vmem(7) + [pl.BlockSpec(memory_space=pltpu.SMEM)],
-        out_specs=pl.BlockSpec(memory_space=pltpu.VMEM),
-        compiler_params=pltpu.CompilerParams(vmem_limit_bytes=LIMIT),
-    )(image, one, two, b, margin, phase, jnp.asarray(gradient_tables()), thresholds)
+    return jnp.maximum(result, 0.0)
 
 
 def solution(mesh):

time: 104 us -> 85.9 us (0.83)
  local copies, waits for them, and re-layouts: 11.8 us -> 0 us
  Pallas kernels: 91.7 us -> 82.6 us
  other arithmetic: 0 us -> 3.14 us
    unnamed x32 -> x0, local copies, waits for them, and re-layouts: 11.1 us -> none
    pallas_call x2 -> x1, Pallas kernels: 91.7 us -> 82.6 us  [on_device(): pl.pallas_call(main_kernel, out_shape=sds(BAND, COLS), in_specs=anywhere(...]
    max x0 -> x1, other arithmetic: none -> 3.14 us  [on_device(): return jnp.maximum(result, 0.0)]
where the time goes in v3:
time: 85.9 us; the launch traced here: 85.7 us
  Pallas kernels  82.6 us (96%)
  other arithmetic  3.14 us (4%)
    pallas_call x1, Pallas kernels, on_device(): pl.pallas_call(main_kernel, out_shape=sds(BAND, COLS), in_specs=anywhere(...  82.6 us
    max x1, other arithmetic, on_device(): return jnp.maximum(result, 0.0)  3.14 us

profile of v3, /device:TPU:1, one launch (start us, length us, event | category | flops | bytes accessed | tf_op | source)
XLA Modules:
  0.0 85.7 jit_solution(4158382635520366240)
XLA Ops:
  0.0 82.6 %shard_map.172 = f32[256,2048]{1,0:T(8,128)} custom-call(f32[256,2048]{1,0:T(8,128)} %image.1, f32[64,32,256]{2,1,0:T(8,128)} %constant.20.clone.waves_all, f32[4,96,128]{2,1,0:T(8,128)} %constant.21.clone.mix_all, f32[32,2,48,256]{3,2,1,0:T(8,128)} %constant.22.clone.twist_all, f32[512,128]{1,0:T(8,128)} %constant.23.clone.last_hbm, ...), custom_call_target="tpu_custom_call" | custom-call | tf_op jit(solution)/shard_map/pallas_call | solution.py:834
  82.6 3.1 %broadcast_maximum_fusion = f32[256,2048]{1,0:T(8,128)} fusion(f32[256,2048]{1,0:T(8,128)} %shard_map.172), kind=kLoop, calls=%fused_computation | loop fusion | flops 524288 | bytes 4194304 | tf_op jit(solution)/shard_map/max | solution.py:875

commit v4 on v3

--- a/solution.py
+++ b/solution.py
@@ -177,6 +177,12 @@
 
 def dot(a, b, precision=None):
     return jnp.dot(a, b, preferred_element_type=f32, precision=precision)
+
+
+def dot3(a, b):
+    a_hi, a_lo = split(a)
+    b_hi, b_lo = split(b)
+    return dot(a_hi, b_hi) + (dot(a_hi, b_lo) + dot(a_lo, b_hi))
 
 
 def position():
@@ -550,7 +556,7 @@
     wide = jnp.concatenate(
         [gathered[pl.ds(0, 128, stride=2), :], gathered[pl.ds(1, 128, stride=2), :]], axis=1
     )
-    mixed = dot(mix[...], wide, HI)
+    mixed = dot3(mix[...], wide)
     cos, sin = twist[0], twist[1]
     turned_a, turned_b = [], []
     for part in range(5):
@@ -564,7 +570,7 @@
     turned = jnp.concatenate(
         [jnp.concatenate(turned_a, axis=0), jnp.concatenate(turned_b, axis=0)], axis=1
     )
-    spec = dot(turned, last[...], HI)
+    spec = dot3(turned, last[...])
     group8 = lax.broadcasted_iota(jnp.int32, (8, 128), 1) // 32
     value = spec[0:8]
     for b_lo in range(1, 4):
@@ -612,7 +618,7 @@
             table_lo[(j + 8) * 32 : (j + 9) * 32, :] = lo
 
     def visit(step):
-        lanes = pl.ds(pl.multiple_of(step * 256, 256), 256)
+        lanes = slice(step * 256, step * 256 + 256)
         chosen = pick[:, lanes]
         col_taps = col_taps_all[:, lanes]
         row_taps = row_taps_all[:, lanes]
@@ -632,7 +638,8 @@
             values_hi[d * 32 : d * 32 + 32, lanes] = hi
             values_lo[d * 32 : d * 32 + 32, lanes] = lo
 
-    loop(VDEV // 256, visit)
+    for step in range(VDEV // 256):
+        visit(step)
 
     def scatter(values):
         return lax.dot_general(
@@ -725,9 +732,9 @@
     stack = jnp.concatenate(rows, axis=0)
     sign = jnp.where(lax.broadcasted_iota(jnp.int32, (8, 256), 0) < 4, -1.0, 1.0)
     operand = jnp.concatenate([stack, rotate(stack, sign)], axis=1)
-    spun = dot(operand, first[...], HI)
+    spun = dot3(operand, first[...])
     spun = spun * turned_back[0] + rotate(spun, sign) * turned_back[1]
-    solved = dot(unmix[...], spun, HI)
+    solved = dot3(unmix[...], spun)
     upper = lax.broadcasted_iota(jnp.int32, (8, 128), 0) < 4
     block2[...] = jnp.where(upper, solved[0:8, 0:128], solved[0:8, 128:256])
     relay = links.spread(block2, blocks2, depth_sem2, local_sem2)
@@ -775,7 +782,7 @@
         c2 = two[:, lanes] - dot(slopes[variant, 2], operands[2][:, lanes])
         d0, d1 = c0 - c1, c1 - c2
         kept = (d0 - jnp.clip(d0, -t0, t0)) + (d1 - jnp.clip(d1, -t1, t1))
-        out[:, lanes] = kept + c2
+        out[:, lanes] = jnp.maximum(kept + c2, 0.0)
         region = pl.ds(tile * 256, 256)
         stores.append(
             pltpu.make_async_copy(out.at[:, region], out_hbm.at[:, region], store_sem.at[tile])
@@ -803,6 +810,25 @@
 
 EXT = COLS + 256
 TALL = BAND + 16
+
+
+def hand_on(result, out, held, sem):
+    regions = [pl.ds(part * 32, 32) for part in range(8)]
+    arriving = [
+        pltpu.make_async_copy(result.at[rows], held.at[rows], sem.at[0, part])
+        for part, rows in enumerate(regions)
+    ]
+    leaving = [
+        pltpu.make_async_copy(held.at[rows], out.at[rows], sem.at[1, part])
+        for part, rows in enumerate(regions)
+    ]
+    for copy in arriving:
+        copy.start()
+    for arrived, copy in zip(arriving, leaving):
+        arrived.wait()
+        copy.start()
+    for copy in leaving:
+        copy.wait()
 
 
 def anywhere(count):
@@ -872,7 +898,14 @@
         jnp.asarray(gradient_tables()), kernel.T, observed, weights[None], row_cell[None],
         col_cell[None], row_offset[None], col_offset[None], thresholds,
     )
-    return jnp.maximum(result, 0.0)
+    return pl.pallas_call(
+        hand_on,
+        out_shape=sds(BAND, COLS),
+        in_specs=[pl.BlockSpec(memory_space=pltpu.HBM)],
+        out_specs=pl.BlockSpec(memory_space=pltpu.HBM),
+        scratch_shapes=[V((BAND, COLS), f32), pairs(8)],
+        compiler_params=pltpu.CompilerParams(vmem_limit_bytes=LIMIT),
+    )(result)
 
 
 def solution(mesh):

time: 85.9 us -> 82.3 us (0.958)
  other arithmetic: 3.14 us -> 0 us
    max x1 -> x0, other arithmetic: 3.14 us -> none  [on_device(): return jnp.maximum(result, 0.0)]
    pallas_call x1, Pallas kernels: 82.6 us -> 79.8 us  [on_device(): pl.pallas_call(main_kernel, out_shape=sds(BAND, COLS), in_specs=anywhere(...]
    pallas_call x0 -> x1, Pallas kernels: none -> 2.4 us  [on_device(): pl.pallas_call(hand_on, out_shape=sds(BAND, COLS), in_specs=[pl.BlockSpec...]
where the time goes in v4:
time: 82.3 us; the launch traced here: 82.2 us
  Pallas kernels  82.2 us (100%)
    pallas_call x1, Pallas kernels, on_device(): pl.pallas_call(main_kernel, out_shape=sds(BAND, COLS), in_specs=anywhere(...  79.8 us
    pallas_call x1, Pallas kernels, on_device(): pl.pallas_call(hand_on, out_shape=sds(BAND, COLS), in_specs=[pl.BlockSpec...  2.4 us

profile of v4, /device:TPU:1, one launch (start us, length us, event | category | flops | bytes accessed | tf_op | source)
XLA Modules:
  0.0 82.2 jit_solution(1652528965202145433)
XLA Ops:
  0.0 79.8 %shard_map.172.result = f32[256,2048]{1,0:T(8,128)} custom-call(f32[256,2048]{1,0:T(8,128)} %image.1, f32[64,32,256]{2,1,0:T(8,128)} %constant.18.clone.waves_all, f32[4,96,128]{2,1,0:T(8,128)} %constant.19.clone.mix_all, f32[32,2,48,256]{3,2,1,0:T(8,128)} %constant.20.clone.twist_all, f32[512,128]{1,0:T(8,128)} %constant.21.clone.last_hbm, ...), custom_call_target="tpu_custom_call" | custom-call | tf_op jit(solution)/shard_map/pallas_call | solution.py:860
  79.8 2.4 %shard_map.173 = f32[256,2048]{1,0:T(8,128)} custom-call(f32[256,2048]{1,0:T(8,128)} %shard_map.172.result), custom_call_target="tpu_custom_call" | custom-call | tf_op jit(solution)/shard_map/pallas_call | solution.py:901

commit v5 on v4

--- a/solution.py
+++ b/solution.py
@@ -873,14 +873,14 @@
             V((256, VDEV), bf16), V((16, VDEV), f32), V((16, VDEV), f32),
             V((480, 256), bf16), V((480, 256), bf16), V((480, VDEV), bf16),
             V((480, VDEV), bf16),
-            V((512, 128), f32), V((384, 128), f32), V((128, 128), f32), V((120, 128), f32),
-            V((8, 128), f32), V((256, 128), f32), V((8, 128), f32), V((512, 128), f32),
+            V((520, 128), f32), V((384, 128), f32), V((128, 128), f32), V((120, 128), f32),
+            V((8, 128), f32), V((264, 128), f32), V((8, 128), f32), V((520, 128), f32),
             V((1, 128), f32), V((16, 1, 128), f32),
             V((2, 8, 256), f32), V((8, 512), f32), V((8, 512), f32),
-            V((512, 128), f32), V((16, 128), f32), V((384, 128), f32), V((3, 16, 128), f32),
+            V((520, 128), f32), V((16, 128), f32), V((384, 128), f32), V((3, 16, 128), f32),
             V((128, 128), f32), V((16, 1, 128), f32), V((120, 128), f32),
             V((15, 1, 128), f32), V((8, 128), f32), V((1, 128), f32),
-            V((256, 128), f32), V((8, 1, 128), f32), V((8, 128), f32), V((512, 128), f32),
+            V((264, 128), f32), V((8, 1, 128), f32), V((8, 128), f32), V((520, 128), f32),
             V((2, 128), f32), V((16, 2, 128), f32),
             pltpu.SemaphoreType.DMA((24,)),
             sems(17), sems(2), sems(2), sems(16), sems(2), sems(2), pairs(8),

time: 82.3 us -> 82.3 us (level)
  no operation moved by 1% of the time
where the time goes in v5:
time: 82.3 us; the launch traced here: 82.2 us
  Pallas kernels  82.1 us (100%)
    pallas_call x1, Pallas kernels, on_device(): pl.pallas_call(main_kernel, out_shape=sds(BAND, COLS), in_specs=anywhere(...  79.8 us
    pallas_call x1, Pallas kernels, on_device(): pl.pallas_call(hand_on, out_shape=sds(BAND, COLS), in_specs=[pl.BlockSpec...  2.4 us

profile of v5, /device:TPU:1, one launch (start us, length us, event | category | flops | bytes accessed | tf_op | source)
XLA Modules:
  0.0 82.2 jit_solution(1562774576901991259)
XLA Ops:
  0.0 79.8 %shard_map.172.result = f32[256,2048]{1,0:T(8,128)} custom-call(f32[256,2048]{1,0:T(8,128)} %image.1, f32[64,32,256]{2,1,0:T(8,128)} %constant.18.clone.waves_all, f32[4,96,128]{2,1,0:T(8,128)} %constant.19.clone.mix_all, f32[32,2,48,256]{3,2,1,0:T(8,128)} %constant.20.clone.twist_all, f32[512,128]{1,0:T(8,128)} %constant.21.clone.last_hbm, ...), custom_call_target="tpu_custom_call" | custom-call | tf_op jit(solution)/shard_map/pallas_call | solution.py:860
  79.8 2.4 %shard_map.173 = f32[256,2048]{1,0:T(8,128)} custom-call(f32[256,2048]{1,0:T(8,128)} %shard_map.172.result), custom_call_target="tpu_custom_call" | custom-call | tf_op jit(solution)/shard_map/pallas_call | solution.py:901
